TPU v7x, 32 devices: a whole 2x2x4 slice. The times are simulated.
32 devices in a mesh: seq: 8 (over z, y), batch: 4 (over x, core).
Axes of the slice: x: 2, y: 2, z: 4, core: 2. Of those that a mesh axis runs over, the one named last changes fastest.
Arguments:
- tokens: bfloat16 [16, 2048, 1024], P('batch', 'seq'), may hold values from -6 to 6
- cotangent: bfloat16 [16, 2048, 1024], P('batch', 'seq'), may hold values from -6 to 6
- log_decay: float32 [16, 2048], P(None, 'seq'), may hold values from -2.6 to 0
- w_mix: float32 [4, 1024, 1024], P(None, 'batch'), may hold values from -0.1875 to 0.1875
- w_out: float32 [1024, 1024], P('batch'), may hold values from -0.25 to 0.25
- w_in: float32 [2, 2816, 1024], P(None, 'batch'), may hold values from -0.1875 to 0.1875
- w_down: float32 [2816, 1024], P('batch'), may hold values from -0.109375 to 0.109375
- m_mix: float32 [4, 1024, 1024], P(None, 'batch'), may hold values from -512 to 512
- m_out: float32 [1024, 1024], P('batch'), may hold values from -512 to 512
- m_in: float32 [2, 2816, 1024], P(None, 'batch'), may hold values from -512 to 512
- m_down: float32 [2816, 1024], P('batch'), may hold values from -512 to 512
Outputs:
- activations: bfloat16 [16, 2048, 1024], P('batch', 'seq')
- input_grad: bfloat16 [16, 2048, 1024], P('batch', 'seq')
- mom_mix: float32 [4, 1024, 1024], P(None, 'batch')
- mom_out: float32 [1024, 1024], P('batch')
- mom_in: float32 [2, 2816, 1024], P(None, 'batch')
- mom_down: float32 [2816, 1024], P('batch')
- new_mix: float32 [4, 1024, 1024], P(None, 'batch')
- new_out: float32 [1024, 1024], P('batch')
- new_in: float32 [2, 2816, 1024], P(None, 'batch')
- new_down: float32 [2816, 1024], P('batch')
- copy_mix: bfloat16 [4, 1024, 1024], P(None, 'batch')
- copy_out: bfloat16 [1024, 1024], P('batch')
- copy_in: bfloat16 [2, 2816, 1024], P(None, 'batch')
- copy_down: bfloat16 [2816, 1024], P('batch')
All inputs are finite; a program needn't handle non-finite values.
Results may differ from a plain program's by a relative error of at most 0.03.
Values may be sent and summed in bfloat16 or wider, within the bound.
No kernel may reach another device: no remote copies, remote signals or barrier semaphores. Data moves between devices by JAX's collectives and lax.ppermute only.
A program may use at most 384 MiB of HBM per device.

v0:
```python
import math

import jax
import jax.numpy as jnp
from jax import lax
from jax.sharding import PartitionSpec as P

D = 1024
HEAD_COUNT = 16
HEAD_DIM = 64
FF = 2816
ITERS = 5


EPSILON = 1e-06
NORM_FLOOR = 1e-07
COEFF_A = 3.4445
COEFF_B = -4.775
COEFF_C = 2.0315
MOMENTUM = 0.5
STEP_RATE = 0.8
PRECISE = lax.Precision.HIGHEST


def carried_in(value, axis, join, neutral):
    place = lax.axis_index(axis)
    gathered = jax.tree.map(
        lambda a, kind: lax.all_gather(a.astype(kind), axis), value, (jnp.bfloat16, jnp.bfloat16)
    )
    state = jax.tree.map(lambda a, e: jnp.zeros_like(a) + jnp.asarray(e, a.dtype), value, neutral)

    def one(turn, state):
        return join(
            state,
            jax.tree.map(
                lambda a, own: lax.dynamic_index_in_dim(a, turn, 0, False).astype(own.dtype),
                gathered,
                value,
            ),
        )

    return lax.fori_loop(0, place, one, state)


def entering(value, axis, combine, identity):
    devices, mine = (lax.axis_size(axis), lax.axis_index(axis))
    everything = jax.tree.map(
        lambda part, kind: lax.all_gather(part.astype(kind), axis),
        value,
        jax.tree.map(lambda a: jnp.bfloat16 if a.dtype == jnp.float32 else a.dtype, value),
    )
    start = jax.tree.map(
        lambda part, zero: jnp.broadcast_to(jnp.asarray(zero, part.dtype), part.shape),
        value,
        identity,
    )

    def turn(k, before):
        at = devices - 1 - k
        reached = at > mine
        new = combine(
            before, jax.tree.map(lambda part, own: part[at].astype(own.dtype), everything, value)
        )
        return jax.tree.map(lambda a, b: jnp.where(reached, a, b), new, before)

    return lax.fori_loop(0, devices, turn, start)


def shortened(value):
    return jax.tree.map(lambda a: a.astype(jnp.bfloat16) if a.dtype == jnp.float32 else a, value)


def normalize(inputs):
    return inputs * lax.rsqrt(jnp.mean(inputs * inputs, axis=-1, keepdims=True) + EPSILON)


def normalize_back(inputs, grad):
    factor = lax.rsqrt(jnp.mean(inputs * inputs, axis=-1, keepdims=True) + EPSILON)
    normed = inputs * factor
    return factor * (grad - normed * jnp.mean(grad * normed, axis=-1, keepdims=True))


def silu_grad(inputs):
    sigma = jax.nn.sigmoid(inputs)
    return sigma * (1.0 + inputs * (1.0 - sigma))


def dot_f32(left, right):
    return jnp.dot(left, right, preferred_element_type=jnp.float32)


def combine(earlier, later):
    return (earlier[0] * later[0], later[0][None, :, None, None] * earlier[1] + later[1])


def iterate_step(gram_cols, first_term, state_cols, wide_first):
    return (
        COEFF_A * state_cols.astype(jnp.float32)
        + COEFF_B * first_term
        + COEFF_C * dot_f32(wide_first, gram_cols)
    ).astype(jnp.bfloat16)


def shards(tokens, cotangent, log_decay, w_mix, w_out, w_in, w_down, m_mix, m_out, m_in, m_down):
    seq_count, group_len, model_width = tokens.shape
    tok_rows = seq_count * group_len
    full_mix, full_out, full_in, full_down = (
        lax.all_gather(w_mix.astype(jnp.bfloat16), "batch", axis=1, tiled=True),
        lax.all_gather(w_out.astype(jnp.bfloat16), "batch", axis=0, tiled=True),
        lax.all_gather(w_in.astype(jnp.bfloat16), "batch", axis=1, tiled=True),
        lax.all_gather(w_down.astype(jnp.bfloat16), "batch", axis=0, tiled=True),
    )
    inputs = tokens.reshape(tok_rows, model_width).astype(jnp.float32)
    normed = normalize(inputs).astype(jnp.bfloat16)
    projected = jnp.einsum("rd,ide->ire", normed, full_mix, preferred_element_type=jnp.float32)
    head_shape = (seq_count, group_len, HEAD_COUNT, HEAD_DIM)
    q_heads = jax.nn.silu(projected[0]).reshape(head_shape)
    k_heads = jax.nn.silu(projected[1]).reshape(head_shape)
    v_heads = projected[2].reshape(head_shape)
    gate_act = jax.nn.silu(projected[3])
    cum_decay = jnp.cumsum(log_decay, axis=1)
    last_cum = cum_decay[:, -1]
    causal = lax.broadcasted_iota(jnp.int32, (group_len, group_len), 0) >= lax.broadcasted_iota(
        jnp.int32, (group_len, group_len), 1
    )
    spread = cum_decay[:, :, None] - cum_decay[:, None, :]
    decay_mask = jnp.where(causal[None], jnp.exp(jnp.where(causal[None], spread, 0.0)), 0.0)
    lead_decay = jnp.exp(cum_decay)
    trail_decay = jnp.exp(last_cum[:, None] - cum_decay)
    group_decay = jnp.exp(last_cum)
    scores = jnp.einsum("bthe,bshe->bhts", q_heads, k_heads, precision=PRECISE) * decay_mask[None]
    summary = jnp.einsum("bshe,hs,bshf->bhef", k_heads, trail_decay, v_heads, precision=PRECISE)
    identity = (jnp.ones_like(group_decay), jnp.zeros_like(summary))
    _, incoming = carried_in((group_decay, summary), "seq", combine, identity)
    attended = jnp.einsum("bhts,bshf->bthf", scores, v_heads, precision=PRECISE)
    attended = attended + jnp.einsum(
        "bthe,ht,bhef->bthf", q_heads, lead_decay, incoming, precision=PRECISE
    )
    attended = attended.reshape(tok_rows, model_width)
    out_norm = normalize(attended)
    hidden = (out_norm * gate_act).astype(jnp.bfloat16)
    middle = inputs + dot_f32(hidden, full_out)
    normed_ffn = normalize(middle).astype(jnp.bfloat16)
    ffn_pair = jnp.einsum("rd,ifd->irf", normed_ffn, full_in, preferred_element_type=jnp.float32)
    product = (ffn_pair[0] * ffn_pair[1]).astype(jnp.bfloat16)
    output = middle + dot_f32(product, full_down)
    activations = output.reshape(seq_count, group_len, model_width).astype(jnp.bfloat16)
    back_grad = cotangent.reshape(tok_rows, model_width)
    grad_down = jnp.einsum("rf,rd->fd", product, back_grad, preferred_element_type=jnp.float32)
    d_product = lax.dot_general(
        back_grad, full_down, (((1,), (1,)), ((), ())), preferred_element_type=jnp.float32
    )
    d_pair = jnp.stack([d_product * ffn_pair[1], d_product * ffn_pair[0]]).astype(jnp.bfloat16)
    grad_in = jnp.einsum("irf,rd->ifd", d_pair, normed_ffn, preferred_element_type=jnp.float32)
    d_normed_ffn = jnp.einsum("irf,ifd->rd", d_pair, full_in, preferred_element_type=jnp.float32)
    d_middle = (back_grad.astype(jnp.float32) + normalize_back(middle, d_normed_ffn)).astype(
        jnp.bfloat16
    )
    grad_out = jnp.einsum("rk,rd->kd", hidden, d_middle, preferred_element_type=jnp.float32)
    d_hidden = lax.dot_general(
        d_middle, full_out, (((1,), (1,)), ((), ())), preferred_element_type=jnp.float32
    )
    d_gate = d_hidden * out_norm * silu_grad(projected[3])
    d_attended = normalize_back(attended, d_hidden * gate_act).reshape(head_shape)
    local_grad = jnp.einsum(
        "bthe,ht,bthf->bhef", q_heads, lead_decay, d_attended, precision=PRECISE
    )
    _, outgoing = entering((group_decay, local_grad), "seq", combine, identity)
    d_scores = (
        jnp.einsum("bthf,bshf->bhts", d_attended, v_heads, precision=PRECISE) * decay_mask[None]
    )
    d_query = jnp.einsum("bhts,bshe->bthe", d_scores, k_heads, precision=PRECISE)
    d_query = d_query + jnp.einsum(
        "bthf,ht,bhef->bthe", d_attended, lead_decay, incoming, precision=PRECISE
    )
    d_key = jnp.einsum("bhts,bthe->bshe", d_scores, q_heads, precision=PRECISE)
    d_key = d_key + jnp.einsum(
        "bshf,hs,bhef->bshe", v_heads, trail_decay, outgoing, precision=PRECISE
    )
    d_value = jnp.einsum("bhts,bthe->bshe", scores, d_attended, precision=PRECISE)
    d_value = d_value + jnp.einsum(
        "bshe,hs,bhef->bshf", k_heads, trail_decay, outgoing, precision=PRECISE
    )
    d_proj = jnp.stack(
        [
            d_query.reshape(tok_rows, model_width) * silu_grad(projected[0]),
            d_key.reshape(tok_rows, model_width) * silu_grad(projected[1]),
            d_value.reshape(tok_rows, model_width),
            d_gate,
        ]
    ).astype(jnp.bfloat16)
    grad_mix = jnp.einsum("rd,ire->ide", normed, d_proj, preferred_element_type=jnp.float32)
    d_normed = jnp.einsum("ire,ide->rd", d_proj, full_mix, preferred_element_type=jnp.float32)
    d_tokens = d_middle.astype(jnp.float32) + normalize_back(inputs, d_normed)
    input_grad = d_tokens.reshape(seq_count, group_len, model_width).astype(jnp.bfloat16)
    summed = (
        lax.psum_scatter(
            grad_mix.astype(jnp.bfloat16), "batch", scatter_dimension=1, tiled=True
        ).astype(jnp.float32),
        lax.psum_scatter(
            grad_out.astype(jnp.bfloat16), "batch", scatter_dimension=0, tiled=True
        ).astype(jnp.float32),
        lax.psum_scatter(
            grad_in.astype(jnp.bfloat16), "batch", scatter_dimension=1, tiled=True
        ).astype(jnp.float32),
        lax.psum_scatter(
            grad_down.astype(jnp.bfloat16), "batch", scatter_dimension=0, tiled=True
        ).astype(jnp.float32),
    )
    summed = (
        lax.psum(summed[0].astype(jnp.bfloat16), "seq").astype(jnp.float32),
        lax.psum(summed[1].astype(jnp.bfloat16), "seq").astype(jnp.float32),
        lax.psum(summed[2].astype(jnp.bfloat16), "seq").astype(jnp.float32),
        lax.psum(summed[3].astype(jnp.bfloat16), "seq").astype(jnp.float32),
    )
    mom_mix = MOMENTUM * m_mix + summed[0]
    mom_out = MOMENTUM * m_out + summed[1]
    mom_in = MOMENTUM * m_in + summed[2]
    mom_down = MOMENTUM * m_down + summed[3]
    matrices = [
        mom_mix[0],
        mom_mix[1],
        mom_mix[2],
        mom_mix[3],
        mom_out,
        mom_in[0],
        mom_in[1],
        mom_down,
    ]
    rough_mats = [
        lax.optimization_barrier(member.astype(jnp.bfloat16)).astype(jnp.float32)
        for member in matrices
    ]
    squares = jnp.stack([jnp.sum(member * member) for member in rough_mats])
    totals = lax.psum(squares, "batch")
    states = [
        (rough_mats[member] / (jnp.sqrt(totals[member]) + NORM_FLOOR)).astype(jnp.bfloat16)
        for member in range(8)
    ]
    col_count = model_width // lax.axis_size("seq")
    offset = lax.axis_index("seq") * col_count
    for number in range(ITERS):
        col_blocks = [lax.dynamic_slice_in_dim(state, offset, col_count, 1) for state in states]
        gram_sum = lax.psum(
            jnp.stack(
                [
                    jnp.einsum(
                        "rc,rd->cd",
                        states[member],
                        col_blocks[member],
                        preferred_element_type=jnp.float32,
                    )
                    for member in range(8)
                ]
            ).astype(jnp.bfloat16),
            "batch",
        )
        first_terms = [dot_f32(states[member], gram_sum[member]) for member in range(8)]
        wide_terms = lax.all_gather(
            shortened(tuple((term.astype(jnp.bfloat16) for term in first_terms))),
            "seq",
            axis=1,
            tiled=True,
        )
        new_blocks = tuple(
            (
                iterate_step(
                    gram_sum[member], first_terms[member], col_blocks[member], wide_terms[member]
                )
                for member in range(8)
            )
        )
        states = list(
            jax.tree.map(
                lambda part, own: part.astype(own.dtype),
                lax.all_gather(shortened(new_blocks), "seq", axis=1, tiled=True),
                new_blocks,
            )
        )
    wide_factor = math.sqrt(FF / D)
    factors = [1.0, 1.0, 1.0, 1.0, 1.0, wide_factor, wide_factor, 1.0]
    masters = [w_mix[0], w_mix[1], w_mix[2], w_mix[3], w_out, w_in[0], w_in[1], w_down]
    updated = [
        masters[member] - STEP_RATE * factors[member] * states[member].astype(jnp.float32)
        for member in range(8)
    ]
    new_mix = jnp.stack(updated[0:4])
    new_out = updated[4]
    new_in = jnp.stack(updated[5:7])
    new_down = updated[7]
    return (
        activations,
        input_grad,
        mom_mix,
        mom_out,
        mom_in,
        mom_down,
        new_mix,
        new_out,
        new_in,
        new_down,
        new_mix.astype(jnp.bfloat16),
        new_out.astype(jnp.bfloat16),
        new_in.astype(jnp.bfloat16),
        new_down.astype(jnp.bfloat16),
    )


def solution(mesh):
    in_specs = (
        P("batch", "seq", None),
        P("batch", "seq", None),
        P(None, "seq"),
        P(None, "batch", None),
        P("batch", None),
        P(None, "batch", None),
        P("batch", None),
        P(None, "batch", None),
        P("batch", None),
        P(None, "batch", None),
        P("batch", None),
    )
    out_specs = (
        P("batch", "seq", None),
        P("batch", "seq", None),
        P(None, "batch", None),
        P("batch", None),
        P(None, "batch", None),
        P("batch", None),
        P(None, "batch", None),
        P("batch", None),
        P(None, "batch", None),
        P("batch", None),
        P(None, "batch", None),
        P("batch", None),
        P(None, "batch", None),
        P("batch", None),
    )
    return jax.shard_map(shards, mesh=mesh, in_specs=in_specs, out_specs=out_specs, check_vma=False)
```

profile of v0, /device:TPU:8, one launch (start us, length us, event | category | flops | bytes accessed | tf_op | source)
XLA Modules:
  0.0 3429.2 jit_solution(4212531288274227669)
XLA Ops:
  21.1 56.0 %all-gather.40.cloned.1.call-done = bf16[4,1024,1024]{1,2,0:T(8,128)(2,1)} async-done(((bf16[4,256,1024]{1,2,0:T(8,128)(2,1)}), bf16[4,1024,1024]{1,2,0:T(8,128)(2,1)}) %all-gather.40.cloned.1.call-update) | async-done | bytes 8388624 | tf_op jit(solution)/shard_map/all_gather | solution.py:108
  210.8 37.5 %all-gather.108.cloned.1.call-done = bf16[32,16,64,64]{3,2,1,0:T(8,128)(2,1)} async-done(((bf16[4,16,64,64]{3,2,1,0:T(8,128)(2,1)}), bf16[32,16,64,64]{3,2,1,0:T(8,128)(2,1)}) %all-gather.108.cloned.1.call-update) | async-done | bytes 4194320 | tf_op jit(solution)/shard_map/all_gather | solution.py:28
  280.9 70.4 %all-gather.44.cloned.1.call-done = bf16[2,2816,1024]{2,1,0:T(8,128)(2,1)} async-done(((bf16[2,704,1024]{2,1,0:T(8,128)(2,1)}), bf16[2,2816,1024]{2,1,0:T(8,128)(2,1)}) %all-gather.44.cloned.1.call-update) | async-done | bytes 11534352 | tf_op jit(solution)/shard_map/all_gather | solution.py:110
  694.3 77.8 %reduce-scatter.9.cloned.1.call-done = bf16[2,704,1024]{2,1,0:T(8,128)(2,1)} async-done(((bf16[2,2816,1024]{2,1,0:T(8,128)(2,1)}), bf16[2,704,1024]{2,1,0:T(8,128)(2,1)}) %reduce-scatter.9.cloned.1.call-update) | async-done | bytes 2883600 | tf_op jit(solution)/shard_map/reduce_scatter | solution.py:203
  772.2 74.2 %reduce-scatter.5.cloned.1.call-done = bf16[4,256,1024]{1,2,0:T(8,128)(2,1)} async-done(((bf16[4,1024,1024]{1,2,0:T(8,128)(2,1)}), bf16[4,256,1024]{1,2,0:T(8,128)(2,1)}) %reduce-scatter.5.cloned.1.call-update) | async-done | bytes 2097168 | tf_op jit(solution)/shard_map/reduce_scatter | solution.py:197
  853.7 229.2 %all-reduce.19.cloned.1.call-done = (bf16[4,256,1024]{1,2,0:T(8,128)(2,1)}, bf16[256,1024]{0,1:T(8,128)(2,1)}, bf16[2,704,1024]{2,1,0:T(8,128)(2,1)}, bf16[704,1024]{1,0:T(8,128)(2,1)}) async-done(((bf16[4,256,1024]{1,2,0:T(8,128)(2,1)}, bf16[256,1024]{0,1:T(8,128)(2,1)}, bf16[2,704,1024]{2,1,0:T(8,128)(2,1)}, bf16[704,1024]{1,0:T(8,128)(2,1)}), (bf16[4,256,1024]{1,2,0:T(8,128)(2,1)}, ...) | async-done | bytes 6946832 | tf_op jit(solution)/shard_map/psum | solution.py:211
  1131.6 51.5 %all-reduce.9.cloned.1.call-done = bf16[8,1024,128]{2,1,0:T(8,128)(2,1)} async-done(((bf16[8,1024,128]{2,1,0:T(8,128)(2,1)}), bf16[8,1024,128]{2,1,0:T(8,128)(2,1)}) %all-reduce.9.cloned.1.call-update) | async-done | bytes 2097168 | tf_op jit(solution)/shard_map/psum | solution.py:244
  1190.3 38.3 %all-gather.48.cloned.1.call-done = bf16[704,1024]{1,0:T(8,128)(2,1)} async-done(((bf16[704,128]{1,0:T(8,128)(2,1)}), bf16[704,1024]{1,0:T(8,128)(2,1)}) %all-gather.48.cloned.1.call-update) | async-done | bytes 1441808 | tf_op jit(solution)/shard_map/all_gather | solution.py:259
  1279.3 33.8 all_gather.280
  1350.0 32.8 all_gather.282
  1481.6 32.9 all_gather.286
  1585.2 51.0 %all-reduce.11.cloned.1.call-done = bf16[8,1024,128]{2,1,0:T(8,128)(2,1)} async-done(((bf16[8,1024,128]{2,1,0:T(8,128)(2,1)}), bf16[8,1024,128]{2,1,0:T(8,128)(2,1)}) %all-reduce.11.cloned.1.call-update) | async-done | bytes 2097168 | tf_op jit(solution)/shard_map/psum | solution.py:244
  1644.6 37.2 %all-gather.60.cloned.1.call-done = bf16[704,1024]{1,0:T(8,128)(2,1)} async-done(((bf16[704,128]{1,0:T(8,128)(2,1)}), bf16[704,1024]{1,0:T(8,128)(2,1)}) %all-gather.60.cloned.1.call-update) | async-done | bytes 1441808 | tf_op jit(solution)/shard_map/all_gather | solution.py:259
  1733.2 33.3 all_gather.296
  2033.2 50.3 %all-reduce.13.cloned.1.call-done = bf16[8,1024,128]{2,1,0:T(8,128)(2,1)} async-done(((bf16[8,1024,128]{2,1,0:T(8,128)(2,1)}), bf16[8,1024,128]{2,1,0:T(8,128)(2,1)}) %all-reduce.13.cloned.1.call-update) | async-done | bytes 2097168 | tf_op jit(solution)/shard_map/psum | solution.py:244
  2091.9 37.2 %all-gather.72.cloned.1.call-done = bf16[704,1024]{1,0:T(8,128)(2,1)} async-done(((bf16[704,128]{1,0:T(8,128)(2,1)}), bf16[704,1024]{1,0:T(8,128)(2,1)}) %all-gather.72.cloned.1.call-update) | async-done | bytes 1441808 | tf_op jit(solution)/shard_map/all_gather | solution.py:259
  2180.3 33.4 all_gather.312
  2376.2 33.6 all_gather.318
  2479.7 51.2 %all-reduce.15.cloned.1.call-done = bf16[8,1024,128]{2,1,0:T(8,128)(2,1)} async-done(((bf16[8,1024,128]{2,1,0:T(8,128)(2,1)}), bf16[8,1024,128]{2,1,0:T(8,128)(2,1)}) %all-reduce.15.cloned.1.call-update) | async-done | bytes 2097168 | tf_op jit(solution)/shard_map/psum | solution.py:244
  2539.2 37.2 %all-gather.84.cloned.1.call-done = bf16[704,1024]{1,0:T(8,128)(2,1)} async-done(((bf16[704,128]{1,0:T(8,128)(2,1)}), bf16[704,1024]{1,0:T(8,128)(2,1)}) %all-gather.84.cloned.1.call-update) | async-done | bytes 1441808 | tf_op jit(solution)/shard_map/all_gather | solution.py:259
  2627.6 33.3 all_gather.328
  2823.0 33.1 all_gather.334
  2926.7 51.0 %all-reduce.17.cloned.1.call-done = bf16[8,1024,128]{2,1,0:T(8,128)(2,1)} async-done(((bf16[8,1024,128]{2,1,0:T(8,128)(2,1)}), bf16[8,1024,128]{2,1,0:T(8,128)(2,1)}) %all-reduce.17.cloned.1.call-update) | async-done | bytes 2097168 | tf_op jit(solution)/shard_map/psum | solution.py:244
  3096.9 33.2 all_gather.344
  (682 shorter events, 2185.1 us)
Async XLA Ops:
  133.6 456.3 %all-gather.110.cloned.1.call-start = ((), (), s32[]{:S(2)}) async-start(), calls=%async_computation.48 | async-start | bytes 9437184 | tf_op jit(solution)/shard_map/all_gather | solution.py:48
  485.8 286.3 %reduce-scatter.9.cloned.1.call-start = ((), (), s32[]{:S(2)}) async-start(), calls=%async_computation.10 | async-start | bytes 14417920 | tf_op jit(solution)/shard_map/reduce_scatter | solution.py:203
  505.1 341.3 %reduce-scatter.5.cloned.1.call-start = ((), (), s32[]{:S(2)}) async-start(), calls=%async_computation.8 | async-start | bytes 10485760 | tf_op jit(solution)/shard_map/reduce_scatter | solution.py:197
  694.2 388.7 %all-reduce.19.cloned.1.call-start = ((), (), s32[]{:S(2)}) async-start(), calls=%async_computation.49 | async-start | bytes 13893632 | tf_op jit(solution)/shard_map/psum | solution.py:211
  846.4 336.6 %all-reduce.9.cloned.1.call-start = ((), (), s32[]{:S(2)}) async-start(), calls=%async_computation.12 | async-start | bytes 4194304 | tf_op jit(solution)/shard_map/psum | solution.py:244
  1188.7 290.2 %all-gather.56.cloned.1.call-start = ((), (), s32[]{:S(2)}) async-start(), calls=%async_computation.17 | async-start | bytes 1622016 | tf_op jit(solution)/shard_map/all_gather | solution.py:259
  1190.1 387.4 %all-gather.50.cloned.1.call-start = ((), (), s32[]{:S(2)}) async-start(), calls=%async_computation.14 | async-start | bytes 1622016 | tf_op jit(solution)/shard_map/all_gather | solution.py:276
  1231.3 348.3 %all-gather.54.cloned.1.call-start = ((), (), s32[]{:S(2)}) async-start(), calls=%async_computation.16 | async-start | bytes 1622016 | tf_op jit(solution)/shard_map/all_gather | solution.py:276
  1279.2 302.5 %all-gather.58.cloned.1.call-start = ((), (), s32[]{:S(2)}) async-start(), calls=%async_computation.18 | async-start | bytes 1622016 | tf_op jit(solution)/shard_map/all_gather | solution.py:276
  1641.9 285.1 %all-gather.68.cloned.1.call-start = ((), (), s32[]{:S(2)}) async-start(), calls=%async_computation.24 | async-start | bytes 1622016 | tf_op jit(solution)/shard_map/all_gather | solution.py:259
  1644.6 380.9 %all-gather.62.cloned.1.call-start = ((), (), s32[]{:S(2)}) async-start(), calls=%async_computation.21 | async-start | bytes 1622016 | tf_op jit(solution)/shard_map/all_gather | solution.py:276
  1684.6 343.0 %all-gather.66.cloned.1.call-start = ((), (), s32[]{:S(2)}) async-start(), calls=%async_computation.23 | async-start | bytes 1622016 | tf_op jit(solution)/shard_map/all_gather | solution.py:276
  1733.1 296.6 %all-gather.70.cloned.1.call-start = ((), (), s32[]{:S(2)}) async-start(), calls=%async_computation.25 | async-start | bytes 1622016 | tf_op jit(solution)/shard_map/all_gather | solution.py:276
  2089.2 284.3 %all-gather.80.cloned.1.call-start = ((), (), s32[]{:S(2)}) async-start(), calls=%async_computation.31 | async-start | bytes 1622016 | tf_op jit(solution)/shard_map/all_gather | solution.py:259
  2091.9 380.0 %all-gather.74.cloned.1.call-start = ((), (), s32[]{:S(2)}) async-start(), calls=%async_computation.28 | async-start | bytes 1622016 | tf_op jit(solution)/shard_map/all_gather | solution.py:276
  2131.9 342.1 %all-gather.78.cloned.1.call-start = ((), (), s32[]{:S(2)}) async-start(), calls=%async_computation.30 | async-start | bytes 1622016 | tf_op jit(solution)/shard_map/all_gather | solution.py:276
  2180.2 295.9 %all-gather.82.cloned.1.call-start = ((), (), s32[]{:S(2)}) async-start(), calls=%async_computation.32 | async-start | bytes 1622016 | tf_op jit(solution)/shard_map/all_gather | solution.py:276
  2539.1 379.8 %all-gather.86.cloned.1.call-start = ((), (), s32[]{:S(2)}) async-start(), calls=%async_computation.35 | async-start | bytes 1622016 | tf_op jit(solution)/shard_map/all_gather | solution.py:276
  2579.2 341.9 %all-gather.90.cloned.1.call-start = ((), (), s32[]{:S(2)}) async-start(), calls=%async_computation.37 | async-start | bytes 1622016 | tf_op jit(solution)/shard_map/all_gather | solution.py:276
  2627.6 295.6 %all-gather.94.cloned.1.call-start = ((), (), s32[]{:S(2)}) async-start(), calls=%async_computation.39 | async-start | bytes 1622016 | tf_op jit(solution)/shard_map/all_gather | solution.py:276
  2983.3 336.2 %all-gather.104.cloned.1.call-start = ((), (), s32[]{:S(2)}) async-start(), calls=%async_computation.45 | async-start | bytes 1622016 | tf_op jit(solution)/shard_map/all_gather | solution.py:259
  2986.0 422.5 %all-gather.98.cloned.1.call-start = ((), (), s32[]{:S(2)}) async-start(), calls=%async_computation.42 | async-start | bytes 1622016 | tf_op jit(solution)/shard_map/all_gather | solution.py:276
  3026.0 382.6 %all-gather.102.cloned.1.call-start = ((), (), s32[]{:S(2)}) async-start(), calls=%async_computation.44 | async-start | bytes 1622016 | tf_op jit(solution)/shard_map/all_gather | solution.py:276
  3096.8 321.7 %all-gather.106.cloned.1.call-start = ((), (), s32[]{:S(2)}) async-start(), calls=%async_computation.46 | async-start | bytes 1622016 | tf_op jit(solution)/shard_map/all_gather | solution.py:276
  (139 other events, 7764.2 us)
Sparse Core Ops, SparseCore 0:
  16.5 60.5 all-gather.39
  124.9 123.3 all-gather.107
  275.1 76.1 all-gather.43
  462.0 123.0 all-gather.109
  622.5 54.8 reduce-scatter.10
  680.0 92.1 reduce-scatter.8
  774.6 71.7 reduce-scatter.4
  851.6 231.2 all-reduce.18
  1131.6 51.3 all-reduce.8
  1326.2 48.7 all-gather.49
  1585.3 50.8 all-reduce.10
  1781.7 48.7 all-gather.61
  1833.1 51.1 all-gather.65
  2033.3 50.2 all-reduce.12
  2228.1 49.7 all-gather.73
  2280.5 49.8 all-gather.77
  2376.3 47.6 all-gather.81
  2479.8 51.0 all-reduce.14
  2726.5 49.5 all-gather.89
  2823.1 48.0 all-gather.93
  2926.8 50.9 all-reduce.16
  3069.4 50.3 all-gather.103
  3121.8 49.0 all-gather.97
  3173.4 49.0 all-gather.101
  (22 shorter events, 948.6 us)
where the time goes:
time: 3450 us; the launch traced here: 3430 us
  blocking collectives  1560 us (45%)
  waiting for transfers between devices  1020 us (30%)
  matrix products  536 us (16%)
  local copies, waits for them, and re-layouts  169 us (5%)
  other arithmetic  116 us (3%)
    all_gather x25, blocking collectives, shards(): lax.all_gather(shortened(new_blocks), 'seq', axis=1, tiled=True)  794 us
    all_gather x25, blocking collectives, shards(): lax.all_gather(shortened(tuple((term.astype(jnp.bfloat16) for term in fir...  743 us
    psum x5, waiting for transfers between devices, shards(): lax.psum(jnp.stack([jnp.einsum('rc,rd->cd', states[member], col_blocks[me...  255 us
    psum x1, waiting for transfers between devices, shards(): lax.psum(summed[0].astype(jnp.bfloat16), 'seq').astype(jnp.float32)  229 us
    all_gather x15, waiting for transfers between devices, shards(): lax.all_gather(shortened(tuple((term.astype(jnp.bfloat16) for term in fir...  193 us
    dot_general x82, matrix products, dot_f32(): return jnp.dot(left, right, preferred_element_type=jnp.float32)  169 us
    reduce_scatter x1, waiting for transfers between devices, shards(): lax.psum_scatter(grad_in.astype(jnp.bfloat16), 'batch', scatter_dimension...  77.8 us
    reduce_scatter x1, waiting for transfers between devices, shards(): lax.psum_scatter(grad_mix.astype(jnp.bfloat16), 'batch', scatter_dimensio...  74.2 us
  transfers between devices with their start and end apart: 46, of which 21 were waited for; matrix products, arithmetic and copies ran while one was open for 18% of the time, Pallas kernels for 0%

commit v1 on v0

v1 whole, which is shorter than its diff:
```python
import math

import jax
import jax.numpy as jnp
from jax import lax
from jax.experimental import pallas as pl
from jax.experimental.pallas import tpu as pltpu
from jax.sharding import PartitionSpec as P

D = 1024
HEAD_COUNT = 16
HEAD_DIM = 64
FF = 2816
ITERS = 5
PAIRS = HEAD_COUNT // 2
LANES = 2 * HEAD_DIM
TILE = 256
HEADS_PER_TILE = TILE // HEAD_DIM
PAIRS_PER_TILE = TILE // LANES
QUADS = 4

EPSILON = 1e-06
NORM_FLOOR = 1e-07
COEFF_A = 3.4445
COEFF_B = -4.775
COEFF_C = 2.0315
MOMENTUM = 0.5
STEP_RATE = 0.8

F32 = jnp.float32
BF16 = jnp.bfloat16
MIB = 1024 * 1024


def dot_nn(left, right):
    return lax.dot_general(left, right, (((1,), (0,)), ((), ())), preferred_element_type=F32)


def dot_nt(left, right):
    return lax.dot_general(left, right, (((1,), (1,)), ((), ())), preferred_element_type=F32)


def dot_tn(left, right):
    return lax.dot_general(left, right, (((0,), (0,)), ((), ())), preferred_element_type=F32)


def silu_grad(inputs):
    sigma = jax.nn.sigmoid(inputs)
    return sigma * (1.0 + inputs * (1.0 - sigma))


def inverse_rms(inputs):
    return lax.rsqrt(jnp.mean(inputs * inputs, axis=-1, keepdims=True) + EPSILON)


def normalize_back(inputs, grad):
    factor = inverse_rms(inputs)
    normed = inputs * factor
    return factor * (grad - normed * jnp.mean(grad * normed, axis=-1, keepdims=True))


def first_half(shape):
    return lax.broadcasted_iota(jnp.int32, shape, len(shape) - 1) < HEAD_DIM


def head_parts(pair):
    low = first_half(pair.shape)
    zero = jnp.zeros_like(pair)
    return (jnp.where(low, pair, zero), jnp.where(low, zero, pair))


def compact(full):
    return jnp.where(first_half((HEAD_DIM, LANES)), full[:HEAD_DIM], full[HEAD_DIM:])


def expand(state):
    return jnp.concatenate(head_parts(state), axis=0)


def params(limit=56):
    return pltpu.CompilerParams(vmem_limit_bytes=limit * MIB)


def cost(flops, nbytes, share=0.1):
    return pl.CostEstimate(flops=int(flops / share), bytes_accessed=int(nbytes / share), transcendentals=0)


def whole(shape):
    return pl.BlockSpec(shape, lambda i: (0,) * len(shape))


def cols(rows, width=TILE):
    return pl.BlockSpec((rows, width), lambda i: (0, i))


def rows_of(rows, width=D):
    return pl.BlockSpec((rows, width), lambda i: (i, 0))


def exact(left, right, dims):
    return lax.dot_general(
        left, right, (dims, ((), ())), preferred_element_type=F32, precision=lax.Precision.HIGHEST
    )


def decay_kernel(log_ref, last_ref, cum_ref, lead_ref, trail_ref, mask_ref, mask_t_ref):
    logs = log_ref[...]
    length = logs.shape[1]
    row = lax.broadcasted_iota(jnp.int32, (length, length), 0)
    col = lax.broadcasted_iota(jnp.int32, (length, length), 1)
    cum = exact(logs, (row <= col).astype(F32), ((1,), (0,)))
    cum_ref[...] = cum
    last = cum[:, length - 1 :]
    last_ref[...] = last
    lane = lax.broadcasted_iota(jnp.int32, (HEAD_COUNT, D), 1) // HEAD_DIM
    spread = (lane == lax.broadcasted_iota(jnp.int32, (HEAD_COUNT, D), 0)).astype(F32)
    lead_ref[...] = jnp.exp(exact(cum, spread, ((0,), (0,))))
    trail_ref[...] = jnp.exp(exact(last - cum, spread, ((0,), (0,))))
    upright = cum.T
    for h in range(HEAD_COUNT):
        span = upright[:, h : h + 1] - cum[h : h + 1, :]
        mask_ref[h] = jnp.where(row >= col, jnp.exp(jnp.minimum(span, 0.0)), 0.0)
        mask_t_ref[h] = jnp.where(col >= row, jnp.exp(jnp.minimum(-span, 0.0)), 0.0)


def factor_kernel(members, place_ref, logs_ref, out_ref):
    logs = logs_ref[...]
    count = logs.shape[0]
    quad, member = place_ref[0], place_ref[1]
    here = quad * members + member
    start, end = quad * members, quad * members + members - 1
    row = lax.broadcasted_iota(jnp.int32, (count, count), 0)
    col = lax.broadcasted_iota(jnp.int32, (count, count), 1)
    before = exact((col < row).astype(F32), logs, ((1,), (0,)))
    through = before + logs
    at_row = lax.broadcasted_iota(jnp.int32, (count, HEAD_COUNT), 0)

    def at(sums, i):
        return jnp.sum(jnp.where(at_row == i, sums, 0.0), axis=0, keepdims=True)

    def factor(log, valid=True):
        return jnp.where(valid, jnp.exp(jnp.minimum(log, 0.0)), 0.0)

    rows = []
    for backward in (False, True):
        for k in range(1, QUADS):
            if backward:
                rows.append(factor(at(before, here + k * members) - at(through, end), quad + k < QUADS))
            else:
                rows.append(factor(at(before, start) - at(through, here - k * members), quad - k >= 0))
        spots = [lax.rem(member + k, members) for k in range(members)]
        for spot in spots:
            there = start + spot
            rows.append(factor(at(through, end) - at(through, there) if backward else at(before, there) - at(before, start)))
        for spot in spots:
            there = start + spot
            if backward:
                rows.append(factor(at(before, here) - at(through, there), spot < member))
            else:
                rows.append(factor(at(before, there) - at(through, here), spot > member))
    lane = lax.broadcasted_iota(jnp.int32, (HEAD_COUNT, D), 1) // HEAD_DIM
    spread = (lane == lax.broadcasted_iota(jnp.int32, (HEAD_COUNT, D), 0)).astype(F32)
    out_ref[...] = exact(jnp.concatenate(rows, axis=0), spread, ((1,), (0,)))


def kv_kernel(seqs, x_ref, w_ref, trail_ref, normed_ref, pk_ref, k_ref, v_ref, state_ref):
    @pl.when(pl.program_id(0) == 0)
    def _():
        inputs = x_ref[...].astype(F32)
        normed_ref[...] = (inputs * inverse_rms(inputs)).astype(BF16)

    normed = normed_ref[...]
    pre_k = dot_nn(normed, w_ref[0])
    keys = pre_k * jax.nn.sigmoid(pre_k)
    values = dot_nn(normed, w_ref[1]).astype(BF16)
    pk_ref[...] = pre_k.astype(BF16)
    k_ref[...] = keys.astype(BF16)
    v_ref[...] = values
    trail = trail_ref[...]
    length = trail.shape[0]
    for b in range(seqs):
        at = slice(b * length, (b + 1) * length)
        scaled = (keys[at] * trail).astype(BF16)
        for p in range(PAIRS_PER_TILE):
            lanes = slice(p * LANES, (p + 1) * LANES)
            state_ref[b, p] = compact(dot_tn(scaled[:, lanes], values[at, lanes])).astype(BF16)


def q_kernel(seqs, normed_ref, w_ref, k_ref, v_ref, mask_ref, pq_ref, q_ref, pg_ref, o_ref):
    normed = normed_ref[...]
    pre_q = dot_nn(normed, w_ref[0])
    pq_ref[...] = pre_q.astype(BF16)
    q_ref[...] = (pre_q * jax.nn.sigmoid(pre_q)).astype(BF16)
    pg_ref[...] = dot_nn(normed, w_ref[1]).astype(BF16)
    length = mask_ref.shape[1]
    for b in range(seqs):
        at = slice(b * length, (b + 1) * length)
        for p in range(PAIRS_PER_TILE):
            lanes = slice(p * LANES, (p + 1) * LANES)
            q_parts = head_parts(q_ref[at, lanes])
            v_parts = head_parts(v_ref[at, lanes])
            keys = k_ref[at, lanes]
            total = jnp.zeros((length, LANES), F32)
            for h in range(2):
                scores = dot_nt(q_parts[h], keys) * mask_ref[2 * p + h]
                total = total + dot_nn(scores.astype(BF16), v_parts[h])
            o_ref[at, lanes] = total


def mid_kernel(o_ref, q_ref, state_ref, lead_ref, pg_ref, x_ref, wo_ref, att_ref, hid_ref, mid_ref, nf_ref):
    scaled = (q_ref[...].astype(F32) * lead_ref[...]).astype(BF16)
    for p in range(PAIRS):
        lanes = slice(p * LANES, (p + 1) * LANES)
        att_ref[:, lanes] = o_ref[:, lanes] + dot_nn(scaled[:, lanes], expand(state_ref[0, p]))
    attended = att_ref[...]
    gate_in = pg_ref[...].astype(F32)
    hidden = (attended * inverse_rms(attended) * gate_in * jax.nn.sigmoid(gate_in)).astype(BF16)
    hid_ref[...] = hidden
    middle = x_ref[...].astype(F32) + dot_nn(hidden, wo_ref[...])
    mid_ref[...] = middle
    nf_ref[...] = (middle * inverse_rms(middle)).astype(BF16)


def ffn_kernel(carry, last, more, cut, place_ref, x_refs, out_refs, buffers, sems):
    nf_buf, cot_buf, w_in_buf, w_down_buf, out_buf, dn_buf, prod_buf, first_buf, second_buf, grad_buf = buffers[:10]
    rows = grad_buf.shape[1]
    if place_ref is None:
        targets = [nf_buf, w_in_buf, cot_buf, w_down_buf]
    else:
        half = rows // 2
        here = pl.ds(pl.multiple_of(place_ref[0] * half, half), half)
        there = pl.ds(pl.multiple_of((1 - place_ref[0]) * half, half), half)
        targets = [nf_buf, w_in_buf.at[:, here], w_in_buf.at[:, there], cot_buf, w_down_buf.at[here], w_down_buf.at[there]]
    needed = len(targets)
    targets = targets + [out_buf, dn_buf][:carry] + ([grad_buf] if more else [])
    loads = [
        pltpu.make_async_copy(source, target, sems.at[i]) for i, (source, target) in enumerate(zip(x_refs, targets))
    ]
    for load in loads:
        load.start()
    sum_bufs = buffers[10:] if last else (out_buf, dn_buf)
    out_copies = [pltpu.make_async_copy(buf, ref, sems.at[9 + i]) for i, (buf, ref) in enumerate(zip(sum_bufs, out_refs))]
    pieces = [pl.ds(0, cut), pl.ds(cut, rows - cut)] if cut else [pl.ds(0, rows)]
    grad_copies = [
        [
            pltpu.make_async_copy(grad_buf.at[i, piece], out_refs[2 + j].at[i], sems.at[11 + 2 * i + j])
            for j, piece in enumerate(pieces)
        ]
        for i in range(3)
    ]
    count = nf_buf.shape[0]
    first_half = 2 if place_ref is None else 3
    step = min(TILE, count)
    for at in [slice(t, t + step) for t in range(0, count, step)]:
        if at.start == 0:
            for load in loads[:first_half]:
                load.wait()
        normed = nf_buf[at, :]
        first = dot_nt(w_in_buf[0], normed)
        second = dot_nt(w_in_buf[1], normed)
        if at.start == 0:
            for load in loads[first_half:needed]:
                load.wait()
        cot = cot_buf[at, :]
        d_product = dot_nt(w_down_buf[...], cot)
        product = (first * second).astype(BF16)
        d_first = (d_product * second).astype(BF16)
        d_second = (d_product * first).astype(BF16)
        prod_buf[:, at] = product
        first_buf[:, at] = d_first
        second_buf[:, at] = d_second
        out = dot_tn(product, w_down_buf[...])
        d_normed = dot_tn(d_first, w_in_buf[0]) + dot_tn(d_second, w_in_buf[1])
        if at.start == 0:
            for load in loads[needed:]:
                load.wait()
        if carry > 0:
            out = out_buf[at, :] + out
        if carry > 1:
            d_normed = dn_buf[at, :] + d_normed
        sum_bufs[0][at, :] = out.astype(sum_bufs[0].dtype)
        sum_bufs[1][at, :] = d_normed.astype(sum_bufs[1].dtype)
    for copy in out_copies:
        copy.start()
    for i, (left, right) in enumerate(((first_buf, nf_buf), (second_buf, nf_buf), (prod_buf, cot_buf))):
        for at in [slice(c, c + TILE) for c in range(0, D, TILE)]:
            grad = dot_nn(left[...], right[:, at])
            if more:
                grad = grad + grad_buf[i, :, at].astype(F32)
            grad_buf[i, :, at] = grad.astype(BF16)
        for copy in grad_copies[i]:
            copy.start()
    for copy in out_copies + [copy for copies in grad_copies for copy in copies]:
        copy.wait()


def ffn(normed, cot, weights, sums=(), last=False, grads=None, cut=0, place=None):
    w_in, w_down = ((w,) if place is None else w for w in weights)
    count, rows = normed.shape[0], sum(part.shape[0] for part in w_down)
    away = pl.BlockSpec(memory_space=pl.ANY)
    kind = BF16 if last else F32
    ins = (normed, *w_in, cot, *w_down, *sums) + (() if grads is None else (grads,))
    places = () if place is None else (place,)
    n_in = len(ins)
    parts = [cut, rows - cut] if cut else [rows]
    n_out = 2 + len(parts)
    has_grads = grads is not None

    def body(*refs):
        place_ref = refs[0] if places else None
        refs = refs[len(places) :]
        outs, buffers = refs[n_in : n_in + n_out], refs[n_in + n_out : -1]
        ffn_kernel(len(sums), last, has_grads, cut, place_ref, refs[:n_in], outs, buffers, refs[-1])

    tokens_by = pltpu.VMEM((count, D), BF16)
    units_by = pltpu.VMEM((rows, count), BF16)
    out, d_normed, *grads = pl.pallas_call(
        body,
        in_specs=[pl.BlockSpec(memory_space=pltpu.SMEM)] * len(places) + [away] * n_in,
        out_specs=[away] * n_out,
        out_shape=[jax.ShapeDtypeStruct((count, D), kind)] * 2
        + [jax.ShapeDtypeStruct((3, part, D), BF16) for part in parts],
        scratch_shapes=[tokens_by, tokens_by, pltpu.VMEM((2, rows, D), BF16), pltpu.VMEM((rows, D), BF16)]
        + [pltpu.VMEM((count, D), F32)] * 2
        + [units_by] * 3
        + [pltpu.VMEM((3, rows, D), BF16)]
        + ([tokens_by] * 2 if last else [])
        + [pltpu.SemaphoreType.DMA((17,))],
        compiler_params=params(60),
        cost_estimate=cost(16 * count * D * rows, 12 * rows * D + 12 * count * D),
        name="ffn",
    )(*places, *ins)
    return (out, d_normed), grads


def gate_back_kernel(
    dn_ref, dn_mate_ref, mid_ref, cot_ref, wo_ref, att_ref, pg_ref, q_ref, lead_ref, *out_refs
):
    dmid_ref, datt_ref, dgate_ref, state_ref = out_refs
    d_normed_ffn = dn_ref[...] + dn_mate_ref[...].astype(F32)
    d_middle = cot_ref[...].astype(F32) + normalize_back(mid_ref[...], d_normed_ffn)
    d_middle = d_middle.astype(BF16)
    dmid_ref[...] = d_middle
    d_hidden = dot_nt(d_middle, wo_ref[...])
    attended = att_ref[...]
    factor = inverse_rms(attended)
    out_norm = attended * factor
    gate_in = pg_ref[...].astype(F32)
    sigma = jax.nn.sigmoid(gate_in)
    dgate_ref[...] = (d_hidden * out_norm * sigma * (1.0 + gate_in * (1.0 - sigma))).astype(BF16)
    grad = d_hidden * gate_in * sigma
    d_att = factor * (grad - out_norm * jnp.mean(grad * out_norm, axis=-1, keepdims=True))
    d_att = d_att.astype(BF16)
    datt_ref[...] = d_att
    scaled = (q_ref[...].astype(F32) * lead_ref[...]).astype(BF16)
    for p in range(PAIRS):
        lanes = slice(p * LANES, (p + 1) * LANES)
        state_ref[0, p] = compact(dot_tn(scaled[:, lanes], d_att[:, lanes])).astype(BF16)


def early_grads_kernel(hid_ref, nf_ref, dmid_ref, dgate_ref, out_grad_ref, gate_grad_ref):
    out_grad_ref[0] = dot_tn(hid_ref[...], dmid_ref[...]).astype(BF16)
    gate_grad_ref[0] = dot_tn(nf_ref[...], dgate_ref[...]).astype(BF16)


def att_back_kernel(
    seqs, q_ref, k_ref, v_ref, da_ref, pq_ref, mask_ref, mask_t_ref, state_ref, lead_ref, nf_ref, *out_refs
):
    dq_ref, dk_ref, dv_ref, grad_ref = out_refs[1:]
    lead = lead_ref[...]
    length = lead.shape[0]
    for b in range(seqs):
        at = slice(b * length, (b + 1) * length)
        for p in range(PAIRS_PER_TILE):
            lanes = slice(p * LANES, (p + 1) * LANES)
            queries, keys, values, d_att = (r[at, lanes] for r in (q_ref, k_ref, v_ref, da_ref))
            q_parts, k_parts, v_parts, d_parts = (head_parts(a) for a in (queries, keys, values, d_att))
            d_q = dot_nt((d_att.astype(F32) * lead[:, lanes]).astype(BF16), expand(state_ref[b, p]))
            d_k = jnp.zeros((length, LANES), F32)
            d_v = jnp.zeros((length, LANES), F32)
            for h in range(2):
                mask, mask_t = mask_ref[2 * p + h], mask_t_ref[2 * p + h]
                d_scores = (dot_nt(d_parts[h], values) * mask).astype(BF16)
                d_scores_t = (dot_nt(v_parts[h], d_att) * mask_t).astype(BF16)
                scores_t = (dot_nt(k_parts[h], queries) * mask_t).astype(BF16)
                d_q = d_q + dot_nn(d_scores, k_parts[h])
                d_k = d_k + dot_nn(d_scores_t, q_parts[h])
                d_v = d_v + dot_nn(scores_t, d_parts[h])
            dq_ref[at, lanes] = (d_q * silu_grad(pq_ref[at, lanes].astype(F32))).astype(BF16)
            dk_ref[at, lanes] = d_k
            dv_ref[at, lanes] = d_v
    grad_ref[0] = dot_tn(nf_ref[...], dq_ref[...]).astype(BF16)


def state_back_kernel(
    seqs, k_ref, v_ref, pk_ref, dk_in_ref, dv_in_ref, state_ref, trail_ref, nf_ref, _, dkv_ref, grad_ref
):
    trail = trail_ref[...]
    length = trail.shape[0]
    for b in range(seqs):
        at = slice(b * length, (b + 1) * length)
        k_scaled = (k_ref[at, :].astype(F32) * trail).astype(BF16)
        v_scaled = (v_ref[at, :].astype(F32) * trail).astype(BF16)
        for p in range(PAIRS_PER_TILE):
            lanes = slice(p * LANES, (p + 1) * LANES)
            state = expand(state_ref[b, p])
            d_k = dk_in_ref[at, lanes] + dot_nt(v_scaled[:, lanes], state)
            d_v = dv_in_ref[at, lanes] + dot_nn(k_scaled[:, lanes], state)
            dkv_ref[0, at, lanes] = (d_k * silu_grad(pk_ref[at, lanes].astype(F32))).astype(BF16)
            dkv_ref[1, at, lanes] = d_v.astype(BF16)
    for i in range(2):
        grad_ref[i] = dot_tn(nf_ref[...], dkv_ref[i]).astype(BF16)


def dots_back_kernel(dq_ref, dg_ref, w_ref, out_ref):
    out_ref[...] = dot_nt(dq_ref[...], w_ref[0]) + dot_nt(dg_ref[...], w_ref[1])


def input_back_kernel(dkv_ref, w_ref, part_ref, x_ref, dmid_ref, out_ref):
    d_normed = part_ref[...] + dot_nt(dkv_ref[0], w_ref[0]) + dot_nt(dkv_ref[1], w_ref[1])
    d_tokens = dmid_ref[...].astype(F32) + normalize_back(x_ref[...].astype(F32), d_normed)
    out_ref[...] = d_tokens.astype(BF16)


def newton_kernel(parts, *refs):
    b_refs, (row_ref, out_ref, rest_ref, g_ref, gb_ref, nb_ref, h_ref, hb_ref, x_ref) = refs[:parts], refs[parts:]
    tiles = [slice(i * TILE, (i + 1) * TILE) for i in range(D // TILE)]

    def right_of(at):
        return slice(at.start, D)

    def mirrored(target, at, part):
        low = part.astype(BF16)
        target[at, right_of(at)] = low
        for other in tiles:
            if other.start > at.start:
                target[other, at] = low[:, other.start - at.start : other.stop - at.start].T

    trace = jnp.zeros((1, 1), F32)
    for at in tiles:
        part = sum(dot_tn(b_ref[:, at], b_ref[:, right_of(at)]) for b_ref in b_refs)
        g_ref[at, right_of(at)] = part
        on_row = lax.broadcasted_iota(jnp.int32, (TILE, TILE), 0)
        on_col = lax.broadcasted_iota(jnp.int32, (TILE, TILE), 1)
        trace = trace + jnp.sum(jnp.where(on_row == on_col, part[:, :TILE], 0.0), keepdims=True)
    inverse = 1.0 / (jnp.sqrt(trace) + NORM_FLOOR)
    x_ref[...] = row_ref[...].astype(F32) * inverse
    scale = inverse * inverse
    for at in tiles:
        gram = g_ref[at, right_of(at)] * scale
        g_ref[at, right_of(at)] = gram
        mirrored(gb_ref, at, gram)

    def polynomial():
        for at in tiles:
            square = dot_nn(gb_ref[at, :], gb_ref[:, right_of(at)])
            mirrored(nb_ref, at, COEFF_B * g_ref[at, right_of(at)] + COEFF_C * square)
        state = x_ref[...]
        x_ref[...] = COEFF_A * state + dot_nn(state.astype(BF16), nb_ref[...])

    @pl.loop(0, ITERS - 1)
    def _(turn):
        polynomial()
        for at in tiles:
            half = COEFF_A * g_ref[at, right_of(at)] + dot_nn(gb_ref[at, :], nb_ref[:, right_of(at)])
            h_ref[at, right_of(at)] = half
            mirrored(hb_ref, at, half)
        for at in tiles:
            gram = COEFF_A * h_ref[at, right_of(at)] + dot_nn(nb_ref[at, :], hb_ref[:, right_of(at)])
            g_ref[at, right_of(at)] = gram
            mirrored(gb_ref, at, gram)

    polynomial()
    own = out_ref.shape[0]
    out_ref[...] = x_ref[:own, :].astype(BF16)
    rest_ref[...] = x_ref[own:, :].astype(BF16)


def newton_rows(every, mine, first):
    rows, own = sum(part.shape[0] for part in every), mine.shape[0]
    return pl.pallas_call(
        lambda *refs: newton_kernel(len(every), *refs),
        out_shape=[jax.ShapeDtypeStruct((first, D), BF16), jax.ShapeDtypeStruct((own - first, D), BF16)],
        grid=(1,),
        in_specs=[whole(part.shape) for part in every] + [whole((own, D))],
        out_specs=[whole((first, D)), whole((own - first, D))],
        scratch_shapes=[
            pltpu.VMEM((D, D), F32),
            pltpu.VMEM((D, D), BF16),
            pltpu.VMEM((D, D), BF16),
            pltpu.VMEM((D, D), F32),
            pltpu.VMEM((D, D), BF16),
            pltpu.VMEM((own, D), F32),
        ],
        compiler_params=params(),
        cost_estimate=cost(2 * D * D * (13 * D + rows + 5 * own), 2 * D * (rows + 2 * own)),
        name="newton",
    )(*every, mine)


class Places:
    def __init__(self):
        self.members = lax.axis_size("seq") // QUADS
        self.chips = lax.axis_size("batch") // 2
        at = lax.axis_index("seq").astype(jnp.uint32)
        self.quad, self.member = at // self.members, at % self.members
        at = lax.axis_index("batch").astype(jnp.uint32)
        self.chip, self.core = at // 2, at % 2

    def level(self, name):
        return {
            "quads": (QUADS, self.quad),
            "members": (self.members, self.member),
            "chips": (self.chips, self.chip),
            "core": (2, self.core),
        }[name]

    def send(self, value, name, k, wrap=True):
        pairs = []
        if name in ("quads", "members"):
            for q in range(QUADS):
                for m in range(self.members):
                    if name == "members":
                        pairs.append((q * self.members + m, q * self.members + (m + k) % self.members))
                    elif wrap or 0 <= q + k < QUADS:
                        pairs.append((q * self.members + m, (q + k) % QUADS * self.members + m))
            return lax.ppermute(value, "seq", pairs)
        for x in range(self.chips):
            for c in range(2):
                to = 2 * x + (c + k) % 2 if name == "core" else (x + k) % self.chips * 2 + c
                pairs.append((2 * x + c, to))
        return lax.ppermute(value, "batch", pairs)

    def pair(self, value):
        pairs = []
        for q in range(QUADS):
            for m in range(self.members):
                pairs.append((q * self.members + m, (q ^ 1) * self.members + m))
        return lax.ppermute(value, "seq", pairs)

    def scattered(self, blocks, name, axis=0):
        count, mine = self.level(name)

        def block(j):
            return lax.dynamic_index_in_dim(blocks, j, axis, False)

        return [block(mine)] + [self.send(block((mine + k) % count), name, k) for k in range(1, count)]

    def scatter(self, blocks, name, axis=0):
        return summed(*self.scattered(blocks, name, axis)).astype(BF16)

    def gather(self, block, name, axis=0):
        count, mine = self.level(name)
        shape = block.shape[:axis] + (count,) + block.shape[axis:]
        result = jnp.zeros(shape, block.dtype)
        result = lax.dynamic_update_index_in_dim(result, block, mine, axis)
        for k in range(1, count):
            part = self.send(block, name, k)
            result = lax.dynamic_update_index_in_dim(result, part, (mine + (count - k)) % count, axis)
        return result

    def far_rows(self, own, after, pair_after, use_after):
        n, rows, _ = own.shape
        split = own.reshape(n, 2, rows // 2, D)
        mine = tied(lax.dynamic_index_in_dim(split, self.quad % 2, 1, False), after)
        far = []
        for k in range(1, self.chips):
            part = tied(self.send(mine, "chips", k), pair_after)
            far.append(tied((part, self.pair(part)), use_after))
        return far


def tied(value, *others):
    return lax.optimization_barrier((value, others))[0]


class Carried:
    def __init__(self, places, local, factors, backward):
        self.places = places
        factors = factors.reshape(-1, PAIRS, 1, LANES)
        self.quad_factors = factors[: QUADS - 1]
        self.spot_factors = factors[QUADS - 1 : QUADS - 1 + places.members]
        self.local_factors = factors[QUADS - 1 + places.members :]
        self.local = local
        sign = -1 if backward else 1
        self.arrived = [places.send(self.local, "quads", sign * k, wrap=False) for k in range(1, QUADS)]

    def finish(self, after=()):
        outer = sum(part.astype(F32) * self.quad_factors[k] for k, part in enumerate(self.arrived))
        local = self.local.astype(F32)
        own = self.spot_factors[0] * outer
        self.sent = [
            tied((self.spot_factors[k] * outer + self.local_factors[k] * local).astype(BF16), after)
            for k in range(1, self.places.members)
        ]
        parts = [self.places.send(part, "members", k) for k, part in enumerate(self.sent, 1)]
        return summed(own, *parts).astype(BF16)


def padded(block, rows):
    return jnp.pad(block, ((0, rows - block.shape[0]), (0, 0)))


def summed(*parts):
    total = parts[0].astype(F32)
    for part in parts[1:]:
        total = total + part.astype(F32)
    return total


class WideSum:
    def __init__(self, places, rows):
        self.places = places
        self.shape = (3, places.members, rows // places.members, D)

    def ordered(self, weights):
        places = self.places
        split = weights.reshape(weights.shape[0], places.members, -1, D)
        parts = [
            lax.dynamic_index_in_dim(split, (places.member + k) % places.members, 1, False)
            for k in range(places.members)
        ]
        return jnp.concatenate(parts, axis=1).astype(BF16)

    def cut(self):
        own = self.shape[2]
        return own if own % 16 == 0 else 0

    def parts(self, grads):
        if len(grads) == 1:
            split = grads[0].reshape(self.shape)
            return split[:, 0], [split[:, k] for k in range(1, self.places.members)]
        split = grads[1].reshape((3, -1) + self.shape[2:])
        if self.places.members == 2:
            return grads[0], [grads[1]]
        return grads[0], [split[:, k] for k in range(self.places.members - 1)]

    def exchange(self, offers):
        return [self.places.send(offer, "members", k + 1) for k, offer in enumerate(offers)]


def place_kernel(members, rows, sources, place_ref, *refs):
    sources_refs, out_ref, sems = refs[:-2], refs[-2], refs[-1]
    quad, member = place_ref[0], place_ref[1]
    copies = []
    for i, (ref, start, k, j) in enumerate(sources):
        q, m = lax.rem(quad + (QUADS - k), QUADS), lax.rem(member + (members - j), members)
        block = sources_refs[ref].at[pl.ds(start, rows)]
        copies.append(pltpu.make_async_copy(block, out_ref.at[q, m], sems.at[i]))
    for copy in copies:
        copy.start()
    for copy in copies:
        copy.wait()


def finish_kernel(members, sources, groups, scales, copies, place_ref, *refs):
    count = len({array for array, _, _ in groups})
    n_blocks = len({ref for ref, _, _, _ in sources})
    block_refs, refs = refs[:n_blocks], refs[n_blocks:]
    base_refs, refs = refs[:count], refs[count:]
    out_refs, refs = refs[:count], refs[count:]
    if copies:
        low_refs, refs = refs[:count], refs[count:]
        block_buf, base_buf, low_buf, sems = refs
    else:
        block_buf, base_buf, sems = refs
    quad, member = place_ref[0], place_ref[1]
    rows = block_buf.shape[2]
    loads = []
    for i, (ref, start, k, j) in enumerate(sources):
        q, m = lax.rem(quad + (QUADS - k), QUADS), lax.rem(member + (members - j), members)
        block = block_refs[ref].at[pl.ds(start, rows)]
        loads.append(pltpu.make_async_copy(block, block_buf.at[q, m], sems.at[0, i]))

    def whole_of(ref, q):
        array, at, _ = groups[q]
        return ref[array] if at is None else ref[array].at[at]

    def used(buf, q):
        return buf.at[q, pl.ds(0, members * groups[q][2])]

    bases = [pltpu.make_async_copy(whole_of(base_refs, q), used(base_buf, q), sems.at[1, q]) for q in range(QUADS)]
    for copy in loads + bases:
        copy.start()
    for copy in loads:
        copy.wait()
    stores = []
    for q in range(QUADS):
        bases[q].wait()
        own = groups[q][2]
        for m in range(members):
            at = slice(m * own, (m + 1) * own)
            value = scales[0] * base_buf[q, at] + scales[1][q] * block_buf[q, m, :own].astype(F32)
            base_buf[q, at] = value
            if copies:
                low_buf[q, at] = value.astype(BF16)
        store = [pltpu.make_async_copy(used(base_buf, q), whole_of(out_refs, q), sems.at[2, q])]
        if copies:
            store.append(pltpu.make_async_copy(used(low_buf, q), whole_of(low_refs, q), sems.at[3, q]))
        for copy in store:
            copy.start()
        stores += store
    for copy in stores:
        copy.wait()


class Blocks:
    def __init__(self, places, rows):
        self.places, self.rows = places, rows
        self.arrays, self.sources = [], []

    def add(self, array, *blocks):
        whole_tiles = all(n % 16 == 0 for n in (self.rows, *(start for start, _, _ in blocks)))
        for start, k, j in blocks:
            self.sources.append((len(self.arrays), start if whole_tiles else 0, k, j))
            if not whole_tiles:
                self.arrays.append(array[start : start + self.rows])
        if whole_tiles:
            self.arrays.append(array)

    def finished(self, arrays, groups, scales, copies=False, late=()):
        places = self.places
        away = pl.BlockSpec(memory_space=pl.ANY)
        outs = [jax.ShapeDtypeStruct(array.shape, F32) for array in arrays]
        lows = [jax.ShapeDtypeStruct(array.shape, BF16) for array in arrays] if copies else []
        if any(own % 16 for _, _, own in groups):
            blocks = self.placed(late)
            parts = [blocks[q, :, :own].reshape(-1, D).astype(F32) * scales[1][q] for q, (_, _, own) in enumerate(groups)]
            results = []
            for i, array in enumerate(arrays):
                mine = [part for part, (at, _, _) in zip(parts, groups) if at == i]
                results.append(scales[0] * array + jnp.stack(mine).reshape(array.shape))
            return results + [result.astype(BF16) for result in results if copies]
        tall = (QUADS, places.members * self.rows, D)
        return pl.pallas_call(
            lambda *refs: finish_kernel(places.members, self.sources, groups, scales, copies, *refs),
            in_specs=[pl.BlockSpec(memory_space=pltpu.SMEM)] + [away] * (len(self.arrays) + len(arrays)),
            out_specs=[away] * (len(outs) + len(lows)),
            out_shape=outs + lows,
            scratch_shapes=[
                pltpu.VMEM((QUADS, places.members, self.rows, D), BF16),
                pltpu.VMEM(tall, F32),
            ]
            + ([pltpu.VMEM(tall, BF16)] if copies else [])
            + [pltpu.SemaphoreType.DMA((4, len(self.sources)))],
            compiler_params=params(),
            name="finish",
        )(jnp.stack([places.quad, places.member]).astype(jnp.int32), *tied(self.arrays, late), *arrays)

    def placed(self, late=()):
        places = self.places
        away = pl.BlockSpec(memory_space=pl.ANY)
        return pl.pallas_call(
            lambda *refs: place_kernel(places.members, self.rows, self.sources, *refs),
            in_specs=[pl.BlockSpec(memory_space=pltpu.SMEM)] + [away] * len(self.arrays),
            out_specs=pl.BlockSpec(memory_space=pltpu.VMEM),
            out_shape=jax.ShapeDtypeStruct((QUADS, places.members, self.rows, D), BF16),
            scratch_shapes=[pltpu.SemaphoreType.DMA((len(self.sources),))],
            compiler_params=params(),
            name="place",
        )(jnp.stack([places.quad, places.member]).astype(jnp.int32), *tied(self.arrays, late))


def own_rows(places, sources, most):
    result = None
    zero = jnp.uint32(0)
    for i, (source, at) in enumerate(sources):
        rows = source.shape[1] // places.members
        part = lax.dynamic_slice(source, (jnp.uint32(at), places.member * rows, zero), (1, rows, D))[0]
        part = padded(part, most)
        result = part if result is None else jnp.where(places.quad == i, part, result)
    return result


def shards(tokens, cotangent, log_decay, w_mix, w_out, w_in, w_down, m_mix, m_out, m_in, m_down):
    places = Places()
    seqs, length, _ = tokens.shape
    count = seqs * length
    state_shape = (seqs, PAIRS, HEAD_DIM, LANES)
    tiles = D // TILE

    cot = cotangent.reshape(count, D)

    def gathered(*rows):
        return lax.all_gather(jnp.stack(rows).astype(BF16), "batch", axis=1, tiled=True)

    full_kv = gathered(w_mix[1], w_mix[2])
    full_qg = gathered(w_mix[0], w_mix[3])
    full_out = gathered(w_out)[0]
    square = jax.ShapeDtypeStruct((HEAD_COUNT, length, length), F32)
    by_lane = jax.ShapeDtypeStruct((length, D), F32)
    last, _, lead, trail, mask, mask_t = pl.pallas_call(
        decay_kernel,
        out_shape=[
            jax.ShapeDtypeStruct((HEAD_COUNT, 1), F32),
            jax.ShapeDtypeStruct((HEAD_COUNT, length), F32),
            by_lane,
            by_lane,
            square,
            square,
        ],
        compiler_params=params(),
        name="decay",
    )(log_decay)
    decays = places.gather(places.gather(last[:, 0], "members"), "quads").reshape(-1, HEAD_COUNT)
    members = places.members
    factors = pl.pallas_call(
        lambda *refs: factor_kernel(members, *refs),
        in_specs=[pl.BlockSpec(memory_space=pltpu.SMEM), pl.BlockSpec(memory_space=pltpu.VMEM)],
        out_shape=jax.ShapeDtypeStruct((2 * (2 * members + QUADS - 1), D), F32),
        compiler_params=params(),
        name="factors",
    )(jnp.stack([places.quad, places.member]).astype(jnp.int32), decays).reshape(2, -1, D)

    x = tokens.reshape(count, D)

    tile_state = pl.BlockSpec((seqs, PAIRS_PER_TILE, HEAD_DIM, LANES), lambda i: (0, i, 0, 0))
    row_state = pl.BlockSpec((1, PAIRS, HEAD_DIM, LANES), lambda i: (i, 0, 0, 0))
    tile_mask = pl.BlockSpec((HEADS_PER_TILE, length, length), lambda i: (i, 0, 0))
    pair_cols = pl.BlockSpec((2, D, TILE), lambda i: (0, 0, i))
    wide = jax.ShapeDtypeStruct((count, D), F32)
    narrow = jax.ShapeDtypeStruct((count, D), BF16)

    normed, pre_k, keys, values, summary = pl.pallas_call(
        lambda *refs: kv_kernel(seqs, *refs),
        grid=(tiles,),
        in_specs=[whole((count, D)), pair_cols, cols(length)],
        out_specs=[whole((count, D)), cols(count), cols(count), cols(count), tile_state],
        out_shape=[narrow, narrow, narrow, narrow, jax.ShapeDtypeStruct(state_shape, BF16)],
        compiler_params=params(),
        cost_estimate=cost(4 * count * D * D, 16 * count * D),
        name="kv",
    )(x, full_kv, trail)
    ahead = Carried(places, summary, factors[0], False)
    incoming = ahead.finish()

    cot_mate = places.send(tied(cot, full_kv), "core", 1)
    wide_sum = WideSum(places, w_down.shape[0])
    w_in_late, w_down_late = tied((w_in, w_down), full_kv)
    in_low, down_low = wide_sum.ordered(w_in_late), wide_sum.ordered(w_down_late[None])[0]

    pre_q, queries, gate_in, inner = pl.pallas_call(
        lambda *refs: q_kernel(seqs, *refs),
        grid=(tiles,),
        in_specs=[whole((count, D)), pair_cols, cols(count), cols(count), tile_mask],
        out_specs=[cols(count)] * 4,
        out_shape=[narrow, narrow, narrow, wide],
        compiler_params=params(),
        cost_estimate=cost(8 * count * D * D, 16 * count * D),
        name="query",
    )(normed, full_qg, keys, values, mask)

    attended, hidden, middle, normed_ffn = pl.pallas_call(
        mid_kernel,
        grid=(seqs,),
        in_specs=[
            rows_of(length),
            rows_of(length),
            row_state,
            whole((length, D)),
            rows_of(length),
            rows_of(length),
            whole((D, D)),
        ],
        out_specs=[rows_of(length)] * 4,
        out_shape=[wide, narrow, wide, narrow],
        compiler_params=params(),
        cost_estimate=cost(2 * count * D * D, 24 * count * D),
        name="middle",
    )(inner, queries, incoming, lead, gate_in, x, full_out)

    nf_mate = places.send(normed_ffn, "core", 1)
    near_weights = (in_low, down_low)
    sums, near_own = ffn(normed_ffn, cot, near_weights, (middle,))
    nf_mate, cot_mate = tied((nf_mate, cot_mate), sums)
    cut = wide_sum.cut()
    mate_sums, near = ffn(nf_mate, cot_mate, near_weights, grads=near_own[0], cut=cut)
    far_down = places.far_rows(down_low[None], full_qg, normed_ffn, mate_sums)
    far_in = places.far_rows(in_low, queries, sums, mate_sums)
    far_weights = [(part, [half[0] for half in down]) for part, down in zip(far_in, far_down)]
    place = (places.quad % 2).astype(jnp.int32).reshape(1)
    near, near_offers = wide_sum.parts(near)
    near_arrived = wide_sum.exchange(near_offers)
    far = []
    for k, weights in enumerate(far_weights):
        mate_sums = tied(mate_sums, near_offers)
        mate_sums, grad = ffn(nf_mate, cot_mate, weights, mate_sums, k == len(far_weights) - 1, place=place)
        far += grad
    out_mate, dn_mate = mate_sums
    dn_mate = places.send(dn_mate, "core", 1)
    for k, weights in enumerate(far_weights):
        sums, far[k] = ffn(normed_ffn, cot, weights, tied(sums, mate_sums), grads=far[k], cut=cut, place=place)
    far = [wide_sum.parts(grads) for grads in far]
    far_arrived = [wide_sum.exchange(offers) for _, offers in far]

    d_middle, d_attended, d_gate, local_grad = pl.pallas_call(
        gate_back_kernel,
        grid=(seqs,),
        in_specs=[
            rows_of(length),
            rows_of(length),
            rows_of(length),
            rows_of(length),
            whole((D, D)),
            rows_of(length),
            rows_of(length),
            rows_of(length),
            whole((length, D)),
        ],
        out_specs=[rows_of(length), rows_of(length), rows_of(length), row_state],
        out_shape=[narrow, narrow, narrow, jax.ShapeDtypeStruct(state_shape, BF16)],
        compiler_params=params(),
        cost_estimate=cost(2 * count * D * D, 16 * count * D),
        name="gate_back",
    )(sums[1], dn_mate, middle, cot, full_out, attended, gate_in, queries, lead)
    behind = Carried(places, local_grad, factors[1], True)
    one_cols = pl.BlockSpec((1, D, TILE), lambda i: (0, 0, i))
    four_grads = jax.ShapeDtypeStruct((4, D, D), BF16)
    out_grad, mix_grads = pl.pallas_call(
        early_grads_kernel,
        grid=(tiles,),
        in_specs=[whole((count, D)), whole((count, D)), cols(count), cols(count)],
        out_specs=[one_cols, pl.BlockSpec((1, D, TILE), lambda i: (3, 0, i))],
        out_shape=[jax.ShapeDtypeStruct((1, D, D), BF16), four_grads],
        compiler_params=params(),
        cost_estimate=cost(4 * count * D * D, 12 * count * D),
        name="early_grads",
    )(hidden, normed, d_middle, d_gate)
    d_attended = tied(d_attended, near_arrived)
    d_query, d_key_part, d_value_part, mix_grads = pl.pallas_call(
        lambda *refs: att_back_kernel(seqs, *refs),
        grid=(tiles,),
        in_specs=[cols(count)] * 5
        + [tile_mask, tile_mask, tile_state, cols(length), whole((count, D)), pl.BlockSpec(memory_space=pl.ANY)],
        out_specs=[cols(count)] * 3 + [pl.BlockSpec((1, D, TILE), lambda i: (2, 0, i))],
        out_shape=[narrow, wide, wide, four_grads],
        input_output_aliases={10: 3},
        compiler_params=params(),
        cost_estimate=cost(8 * count * D * D, 20 * count * D),
        name="attention_back",
    )(queries, keys, values, d_attended, pre_q, mask, mask_t, incoming, lead, normed, mix_grads)

    def scattered(grads):
        return lax.psum_scatter(grads, "batch", scatter_dimension=1, tiled=True)

    def members_sum(grads):
        n, rows, _ = grads.shape
        return places.scatter(grads.reshape(n, places.members, rows // places.members, D), "members", 1)

    sum_out = scattered(out_grad)
    far_sums = [
        tied(summed(own, *arrived).astype(BF16), d_query) for (own, _), arrived in zip(far, far_arrived)
    ]
    chip_arrived = [places.send(part, "chips", -(k + 1)) for k, part in enumerate(far_sums)]
    outgoing = behind.finish((d_query, far_sums, sum_out))
    out_mate = places.send(tied(out_mate, d_query), "core", 1)
    sum_out = members_sum(tied(sum_out, behind.sent))[0]
    outgoing = tied(outgoing, sum_out)
    d_normed_part = pl.pallas_call(
        dots_back_kernel,
        grid=(seqs,),
        in_specs=[rows_of(length), rows_of(length), whole((2, D, D))],
        out_specs=rows_of(length),
        out_shape=wide,
        compiler_params=params(),
        cost_estimate=cost(4 * count * D * D, 10 * count * D),
        name="normed_back",
    )(*tied((d_query, d_gate), behind.sent), full_qg)
    outgoing = tied(outgoing, d_normed_part)

    d_kv, mix_grads = pl.pallas_call(
        lambda *refs: state_back_kernel(seqs, *refs),
        grid=(tiles,),
        in_specs=[cols(count)] * 5
        + [tile_state, cols(length), whole((count, D)), pl.BlockSpec(memory_space=pl.ANY)],
        out_specs=[pl.BlockSpec((2, count, TILE), lambda i: (0, 0, i)), pair_cols],
        out_shape=[jax.ShapeDtypeStruct((2, count, D), BF16), four_grads],
        input_output_aliases={8: 1},
        compiler_params=params(),
        cost_estimate=cost(5 * count * D * D, 18 * count * D),
        name="state_back",
    )(keys, values, pre_k, d_key_part, d_value_part, outgoing, trail, normed, mix_grads)
    wide_total = summed(near, *near_arrived, *chip_arrived).astype(BF16)
    sum_out = padded(sum_out, w_down.shape[0] // places.members)
    wide_blocks = jnp.stack([wide_total[2], wide_total[0], wide_total[1], sum_out])
    wide_parts = places.scattered(wide_blocks, "quads")
    mix_sums = scattered(tied(mix_grads, chip_arrived))
    activations = (tied(sums[0], wide_blocks) + out_mate.astype(F32)).astype(BF16)
    d_kv = tied(d_kv, wide_blocks)

    input_grad = pl.pallas_call(
        input_back_kernel,
        grid=(seqs,),
        in_specs=[
            pl.BlockSpec((2, length, D), lambda i: (0, i, 0)),
            whole((2, D, D)),
            rows_of(length),
            rows_of(length),
            rows_of(length),
        ],
        out_specs=rows_of(length),
        out_shape=narrow,
        compiler_params=params(),
        cost_estimate=cost(4 * count * D * D, 16 * count * D),
        name="input_back",
    )(d_kv, full_kv, d_normed_part, x, d_middle).reshape(tokens.shape)

    wide_mom = ((m_down[None], 0), (m_in, 0), (m_in, 1), (m_out[None], 0))
    mix_mom = [(m_mix, i) for i in range(4)]

    def momentum_rows(sources, grad, after):
        arrays = tied([array for array, _ in sources], after)
        own = own_rows(places, [(array, at) for array, (_, at) in zip(arrays, sources)], grad.shape[0])
        return (MOMENTUM * own + grad.astype(F32)).astype(BF16)

    def to_members(part):
        return [places.send(part, "members", j) for j in range(1, places.members)]

    mix_split = tied(mix_sums, (input_grad, wide_parts)).reshape(4, places.members, -1, D)
    mix_offers = [
        lax.dynamic_index_in_dim(mix_split, (places.member + j) % places.members, 1, False)
        for j in range(places.members)
    ]
    mix_arrived = [places.send(part, "members", j) for j, part in enumerate(mix_offers[1:], 1)]
    wide_grad = summed(*tied(wide_parts, (activations, mix_offers))).astype(BF16)

    wide_low = momentum_rows(wide_mom, wide_grad, wide_blocks)
    wide_known = [wide_low] + to_members(wide_low)
    wide_far = [places.send(wide_low, "chips", k) for k in range(1, places.chips)]
    wide_first = places.send(tied(wide_grad, wide_low), "quads", 1)
    mix_sums = summed(*tied([mix_offers[0]] + mix_arrived, wide_low)).astype(BF16)
    mix_blocks = tied(jnp.stack([mix_sums[i] for i in (2, 0, 1, 3)]), wide_far)
    mix_parts = places.scattered(mix_blocks, "quads")
    mix_grad = summed(*mix_parts).astype(BF16)
    wide_last = [other for part in wide_far for other in to_members(part)]
    wide_known, wide_far = tied((wide_known, wide_far), (mix_parts, wide_last))
    wide_core = jnp.concatenate(wide_known + wide_far, axis=0)
    wide_every = [wide_core, places.send(wide_core, "core", 1)] + wide_last
    wide_every += [places.send(part, "core", 1) for part in wide_last]

    mix_low = momentum_rows(mix_mom, mix_grad, wide_blocks)
    rows, own = wide_grad.shape[0], mix_grad.shape[0]
    mix_others = to_members(jnp.concatenate([mix_low, mix_grad], axis=0))
    mix_known = jnp.concatenate([mix_low] + [part[:own] for part in mix_others], axis=0)
    mix_every = lax.all_gather(mix_known, "batch", axis=0, tiled=True)

    wide_all, mix_all = Blocks(places, rows), Blocks(places, own)
    wide_all.add(wide_grad, (0, 0, 0))
    wide_all.add(wide_first, (0, 1, 0))
    mix_all.add(mix_grad, (0, 0, 0))
    for j, part in enumerate(mix_others, 1):
        mix_all.add(part, (own, 0, j))
    both = jnp.concatenate([wide_grad, mix_grad], axis=0)
    mix_first = places.send(tied(mix_grad, mix_low), "quads", 1)
    both = tied(both, (mix_low, mix_first))
    second, third = (places.send(both, "quads", k) for k in (2, 3))
    early = jnp.concatenate(tied([wide_grad, wide_first], mix_known), axis=0)
    early_arrived = to_members(early)
    for j, part in enumerate(early_arrived, 1):
        wide_all.add(part, (0, 0, j), (rows, 1, j))

    wide_rows, wide_rest = newton_rows(tied(wide_every, (early, mix_known)), wide_core[: rows * places.members], rows)
    wide_x, mix_x = Blocks(places, rows), Blocks(places, own)
    wide_x.add(wide_rows, (0, 0, 0))
    wide_x.add(wide_rest, *[((j - 1) * rows, 0, j) for j in range(1, places.members)])
    x_sent = tied(wide_rows, mix_every)
    x_parts = [places.send(x_sent, "quads", k) for k in (1, 2)]
    mix_rows, mix_rest = newton_rows([tied(mix_every, (wide_rows, early_arrived))], mix_known, own)
    later = jnp.concatenate(tied([second, third, mix_first], mix_rows), axis=0)
    wide_all.add(second, (0, 2, 0))
    wide_all.add(third, (0, 3, 0))
    mix_all.add(mix_first, (0, 1, 0))
    mix_all.add(second, (rows, 2, 0))
    mix_all.add(third, (rows, 3, 0))
    for j, part in enumerate(to_members(later), 1):
        step = rows + own
        wide_all.add(part, (0, 2, j), (step, 3, j))
        mix_all.add(part, (2 * step, 1, j), (rows, 2, j), (step + rows, 3, j))
    x_parts.append(places.send(tied(x_sent, mix_rows), "quads", 3))
    for k, part in enumerate(x_parts, 1):
        wide_x.add(part, (0, k, 0))
    x_pair = jnp.concatenate(tied(x_parts[:2], mix_rows), axis=0)
    x_arrived = to_members(x_pair)
    for j, part in enumerate(x_arrived, 1):
        wide_x.add(part, (0, 1, j), (rows, 2, j))
    mix_x.add(mix_rows, (0, 0, 0))
    mix_x.add(mix_rest, *[((j - 1) * own, 0, j) for j in range(1, places.members)])
    mix_sent = tied(mix_rows, (x_pair, x_parts[2]))
    mix_parts = [places.send(mix_sent, "quads", k) for k in (1, 2, 3)]
    x_last = to_members(x_parts[2])
    for j, part in enumerate(x_last, 1):
        wide_x.add(part, (0, 3, j))
    for k, part in enumerate(mix_parts, 1):
        mix_x.add(part, (0, k, 0))
    for j, part in enumerate(to_members(jnp.concatenate(tied(mix_parts, x_last), axis=0)), 1):
        mix_x.add(part, *[((k - 1) * own, k, j) for k in (1, 2, 3)])

    hidden_rows, width_rows = w_down.shape[0] // places.members, w_out.shape[0] // places.members
    wide_groups = [(0, None, hidden_rows), (1, 0, hidden_rows), (1, 1, hidden_rows), (2, None, width_rows)]
    mix_groups = [(0, i, width_rows) for i in range(4)]
    ones = [1.0] * 4
    mom_down, mom_in, mom_out = wide_all.finished(
        (m_down, m_in, m_out), wide_groups, (MOMENTUM, ones), late=x_last
    )
    (mom_mix,) = mix_all.finished((m_mix,), mix_groups, (MOMENTUM, ones), late=x_last)
    factor = math.sqrt(FF / D)
    steps = [-STEP_RATE, -STEP_RATE * factor, -STEP_RATE * factor, -STEP_RATE]
    new_down, new_in, new_out, copy_down, copy_in, copy_out = wide_x.finished(
        (w_down, w_in, w_out), wide_groups, (1.0, steps), True, late=(mom_down, mom_in, mom_out, mom_mix)
    )
    new_mix, copy_mix = mix_x.finished((w_mix,), mix_groups, (1.0, [-STEP_RATE] * 4), True, late=new_in)
    return (
        activations.reshape(tokens.shape),
        input_grad,
        mom_mix,
        mom_out,
        mom_in,
        mom_down,
        new_mix,
        new_out,
        new_in,
        new_down,
        copy_mix,
        copy_out,
        copy_in,
        copy_down,
    )


def solution(mesh):
    batch_rows = P(None, "batch", None)
    flat_rows = P("batch", None)
    block = P("batch", "seq", None)
    four = (batch_rows, flat_rows, batch_rows, flat_rows)
    in_specs = (block, block, P(None, "seq")) + four + four
    out_specs = (block, block) + four + four + four
    return jax.shard_map(shards, mesh=mesh, in_specs=in_specs, out_specs=out_specs, check_vma=False)
```

time: 3450 us -> 728 us (0.21)
  blocking collectives: 1560 us -> 0 us
  waiting for transfers between devices: 1020 us -> 279 us
  matrix products: 536 us -> 0 us
  Pallas kernels: 0 us -> 299 us
  local copies, waits for them, and re-layouts: 169 us -> 29.6 us
  other arithmetic: 116 us -> 34 us
  starting transfers between devices: 3.18 us -> 65.8 us
    all_gather x50 -> x0, blocking collectives: 1540 us -> none  [the longest x25 794 us: shards(): lax.all_gather(shortened(new_blocks), 'seq', axis=1, tiled=True)]
    dot_general x144 -> x0, matrix products: 536 us -> none  [the longest x82 169 us: dot_f32(): return jnp.dot(left, right, preferred_element_type=jnp.float32)]
    psum x6 -> x0, waiting for transfers between devices: 484 us -> none  [the longest x5 255 us: shards(): lax.psum(jnp.stack([jnp.einsum('rc,rd->cd', states[member], col_blocks[me...]
    all_gather x36 -> x4, waiting for transfers between devices: 382 us -> 30.1 us  [the longest x3 30.1 us: gathered(): lax.all_gather(jnp.stack(rows).astype(BF16), 'batch', axis=1, tiled=True)]
    pallas_call x0 -> x21, Pallas kernels: none -> 299 us  [the longest x4 79.2 us: ffn(): pl.pallas_call(body, in_specs=[pl.BlockSpec(memory_space=pltpu.SMEM)] * l...]
    ppermute x0 -> x52, waiting for transfers between devices: none -> 242 us  [the longest x40 207 us: send(): return lax.ppermute(value, 'seq', pairs)]
    reduce_scatter x4 -> x2, waiting for transfers between devices: 152 us -> 7 us  [scattered(): return lax.psum_scatter(grads, 'batch', scatter_dimension=1, tiled=True)]
    ppermute x0 -> x52, starting transfers between devices: none -> 65.2 us  [the longest x40 60.5 us: send(): return lax.ppermute(value, 'seq', pairs)]
  transfers between devices with their start and end apart: 46 -> 58, of which waited for: 21 -> 33; matrix products, arithmetic and copies ran while one was open for 18% -> 6% of each run, Pallas kernels for 0% -> 41%
where the time goes in v1:
time: 728 us; the launch traced here: 723 us
  Pallas kernels  299 us (41%)
  waiting for transfers between devices  279 us (38%)
  starting transfers between devices  65.8 us (9%)
  other arithmetic  34 us (5%)
  local copies, waits for them, and re-layouts  29.6 us (4%)
  between operations  15.2 us (2%)
    ppermute x40, waiting for transfers between devices, send(): return lax.ppermute(value, 'seq', pairs)  207 us
    pallas_call x4, Pallas kernels, ffn(): pl.pallas_call(body, in_specs=[pl.BlockSpec(memory_space=pltpu.SMEM)] * l...  79.2 us
    pallas_call x2, Pallas kernels, newton_rows(): pl.pallas_call(lambda *refs: newton_kernel(len(every), *refs), out_shape=...  64.5 us
    ppermute x40, starting transfers between devices, send(): return lax.ppermute(value, 'seq', pairs)  60.5 us
    all_gather x3, waiting for transfers between devices, gathered(): lax.all_gather(jnp.stack(rows).astype(BF16), 'batch', axis=1, tiled=True)  30.1 us
    pallas_call x4, Pallas kernels, finished(): pl.pallas_call(lambda *refs: finish_kernel(places.members, self.sources,...  29.7 us
    ppermute x10, waiting for transfers between devices, send(): return lax.ppermute(value, 'batch', pairs)  24.1 us
    pallas_call x1, Pallas kernels, shards(): pl.pallas_call(lambda *refs: att_back_kernel(seqs, *refs), grid=(tiles,),...  22.8 us
  transfers between devices with their start and end apart: 58, of which 33 were waited for; matrix products, arithmetic and copies ran while one was open for 6% of the time, Pallas kernels for 41%

profile of v1, /device:TPU:8, one launch (start us, length us, event | category | flops | bytes accessed | tf_op | source)
XLA Modules:
  0.0 722.6 jit_solution(8568404500480130981)
XLA Ops:
  33.5 13.1 %all-gather.6.cloned.1.call-done.refs_1_.w_ref = bf16[2,1024,1024]{2,1,0:T(8,128)(2,1)} async-done(((bf16[2,256,1024]{2,1,0:T(8,128)(2,1)}), bf16[2,1024,1024]{2,1,0:T(8,128)(2,1)}) %all-gather.6.cloned.1.call-update) | async-done | bytes 4194320 | tf_op jit(solution)/shard_map/all_gather | solution.py:785
  66.2 17.0 %all-gather.8.cloned.1.call-done.refs_1_.w_ref = bf16[2,1024,1024]{2,1,0:T(8,128)(2,1)} async-done(((bf16[2,256,1024]{2,1,0:T(8,128)(2,1)}), bf16[2,1024,1024]{2,1,0:T(8,128)(2,1)}) %all-gather.8.cloned.1.call-update) | async-done | bytes 4194320 | tf_op jit(solution)/shard_map/all_gather | solution.py:785
  83.8 15.9 %query.1 = (bf16[1024,1024]{1,0:T(8,128)(2,1)}, bf16[1024,1024]{1,0:T(8,128)(2,1)}, bf16[1024,1024]{1,0:T(8,128)(2,1)}, f32[1024,1024]{1,0:T(8,128)}) custom-call(bf16[1024,1024]{1,0:T(8,128)(2,1)} %get-tuple-element.168.refs_0_.nf_ref.refs_9_.refs_7_, bf16[2,1024,1024]{2,1,0:T(8,128)(2,1)} %all-gather.8.cloned.1.call-done.refs_1_.w_ref, ...), custom_call_target="tpu_custom_call" | custom-call | flops 85899345920 | bytes 167772160 | tf_op jit(solution)/shard_map/query/pallas_call | solution.py:842
  121.3 11.6 %middle.1 = (f32[1024,1024]{1,0:T(8,128)}, bf16[1024,1024]{1,0:T(8,128)(2,1)}, f32[1024,1024]{1,0:T(8,128)}, bf16[1024,1024]{1,0:T(8,128)(2,1)}) custom-call(f32[1024,1024]{1,0:T(8,128)} %get-tuple-element.172.o_ref, bf16[1024,1024]{1,0:T(8,128)(2,1)} %get-tuple-element.173.q_ref.refs_0_, bf16[4,8,64,128]{3,2,1,0:T(8,128)(2,1)} %add_convert_fusion.7.state_ref.refs_7_, ...), custom_call_target="tpu_custom_call" | custom-call | flops 21474836480 | bytes 251658240 | tf_op jit(solution)/shard_map/middle/pallas_call | solution.py:853
  133.1 19.5 %ffn.4 = (f32[1024,1024]{1,0:T(8,128)}, f32[1024,1024]{1,0:T(8,128)}, bf16[3,704,1024]{2,1,0:T(8,128)(2,1)}) custom-call(bf16[1024,1024]{1,0:T(8,128)(2,1)} %get-tuple-element.178.refs_0_.refs_1_, bf16[2,704,1024]{2,1,0:T(8,128)(2,1)} %copy-done.4, bf16[1024,1024]{1,0:T(8,128)(2,1)} %bitcast.21.refs_2_.refs_4_.cot_ref, ...), custom_call_target="tpu_custom_call" | custom-call | flops 118111600640 | bytes 212336640 | tf_op jit(solution)/shard_map/ffn/pallas_call | solution.py:317
  156.0 18.8 %ffn.5 = (f32[1024,1024]{1,0:T(8,128)}, f32[1024,1024]{1,0:T(8,128)}, bf16[3,352,1024]{2,1,0:T(8,128)(2,1)}, bf16[3,352,1024]{2,1,0:T(8,128)(2,1)}) custom-call(bf16[1024,1024]{1,0:T(8,128)(2,1)} %copy-done.40, bf16[2,704,1024]{2,1,0:T(8,128)(2,1)} %copy-done.4, bf16[1024,1024]{1,0:T(8,128)(2,1)} %collective-permute-done.11.refs_2_.refs_4_, ...), custom_call_target="tpu_custom_call" | custom-call | flops 118111600640 | bytes 212336640 | tf_op jit(solution)/shard_map/ffn/pallas_call | solution.py:317
  187.9 19.7 %ffn.6 = (bf16[1024,1024]{1,0:T(8,128)(2,1)}, bf16[1024,1024]{1,0:T(8,128)(2,1)}, bf16[3,704,1024]{2,1,0:T(8,128)(2,1)}) custom-call(s32[1]{0:T(128)} %bitcast.refs_0_, bf16[1024,1024]{1,0:T(8,128)(2,1)} %copy-done.40, bf16[2,352,1024]{2,1,0:T(8,128)(2,1)} %collective-permute-done.8.refs_2_, bf16[2,352,1024]{2,1,0:T(8,128)(2,1)} %copy-done.42, ...), custom_call_target="tpu_custom_call" | custom-call | flops 118111600640 | bytes 212336640 | tf_op jit(solution)/shard_map/ffn/pallas_call | solution.py:317
  207.7 21.2 %ffn.7 = (f32[1024,1024]{1,0:T(8,128)}, f32[1024,1024]{1,0:T(8,128)}, bf16[3,352,1024]{2,1,0:T(8,128)(2,1)}, bf16[3,352,1024]{2,1,0:T(8,128)(2,1)}) custom-call(s32[1]{0:T(128)} %bitcast.refs_0_, bf16[1024,1024]{1,0:T(8,128)(2,1)} %get-tuple-element.178.refs_0_.refs_1_, bf16[2,352,1024]{2,1,0:T(8,128)(2,1)} %collective-permute-done.8.refs_2_, ...), custom_call_target="tpu_custom_call" | custom-call | flops 118111600640 | bytes 212336640 | tf_op jit(solution)/shard_map/ffn/pallas_call | solution.py:317
  231.9 14.1 %gate_back.1 = (bf16[1024,1024]{1,0:T(8,128)(2,1)}, bf16[1024,1024]{1,0:T(8,128)(2,1)}, bf16[1024,1024]{1,0:T(8,128)(2,1)}, bf16[4,8,64,128]{3,2,1,0:T(8,128)(2,1)}) custom-call(f32[1024,1024]{1,0:T(8,128)} %get-tuple-element.210.dn_ref, bf16[1024,1024]{1,0:T(8,128)(2,1)} %copy-done.41, f32[1024,1024]{1,0:T(8,128)} %get-tuple-element.182.refs_4_.mid_ref, ...), custom_call_target="tpu_custom_call" | custom-call | flops 21474836480 | bytes 167772160 | tf_op jit(solution)/shard_map/gate_back/pallas_call | solution.py:896
  261.9 22.8 %attention_back.1 = (bf16[1024,1024]{1,0:T(8,128)(2,1)}, f32[1024,1024]{1,0:T(8,128)}, f32[1024,1024]{1,0:T(8,128)}, bf16[4,1024,1024]{2,1,0:T(8,128)(2,1)}) custom-call(bf16[1024,1024]{1,0:T(8,128)(2,1)} %get-tuple-element.173.q_ref.refs_0_, bf16[1024,1024]{1,0:T(8,128)(2,1)} %get-tuple-element.169.refs_2_.refs_1_.refs_0_, ...), custom_call_target="tpu_custom_call", output_to_operand_aliasing={{3}: (10, {})} | custom-call | flops 85899345920 | bytes 209715200 | tf_op jit(solution)/shard_map/attention_back/pallas_call | solution.py:930
  319.4 12.7 %state_back.1 = (bf16[2,1024,1024]{2,1,0:T(8,128)(2,1)}, bf16[4,1024,1024]{2,1,0:T(8,128)(2,1)}) custom-call(bf16[1024,1024]{1,0:T(8,128)(2,1)} %get-tuple-element.169.refs_2_.refs_1_.refs_0_, bf16[1024,1024]{1,0:T(8,128)(2,1)} %get-tuple-element.170.refs_3_.refs_2_.refs_1_, ...), custom_call_target="tpu_custom_call", output_to_operand_aliasing={{1}: (8, {})} | custom-call | flops 53687091200 | bytes 188743680 | tf_op jit(solution)/shard_map/state_back/pallas_call | solution.py:971
  354.8 11.0 %input_back.1 = bf16[1024,1024]{1,0:T(8,128)(2,1)} custom-call(bf16[2,1024,1024]{2,1,0:T(8,128)(2,1)} %get-tuple-element.237.dkv_ref, bf16[2,1024,1024]{2,1,0:T(8,128)(2,1)} %all-gather.6.cloned.1.call-done.refs_1_.w_ref, f32[1024,1024]{1,0:T(8,128)} %normed_back.1.part_ref, bf16[1024,1024]{1,0:T(8,128)(2,1)} %bitcast.141, ...), custom_call_target="tpu_custom_call" | custom-call | flops 42949672960 | bytes 167772160 | tf_op jit(solution)/shard_map/input_back/pallas_call | solution.py:991
  365.7 29.2 %collective-permute-done.24 = bf16[352,1024]{1,0:T(8,128)(2,1)S(1)} collective-permute-done((bf16[352,1024]{1,0:T(8,128)(2,1)S(1)}, bf16[352,1024]{1,0:T(8,128)(2,1)S(1)}, u32[]{:S(2)}, u32[]{:S(2)}) %collective-permute-start.24) | collective-permute-done | bytes 720928 | tf_op jit(solution)/shard_map/ppermute | solution.py:527
  394.9 14.3 %collective-permute-done.25 = bf16[352,1024]{1,0:T(8,128)(2,1)S(1)} collective-permute-done((bf16[352,1024]{1,0:T(8,128)(2,1)S(1)}, bf16[352,1024]{1,0:T(8,128)(2,1)S(1)}, u32[]{:S(2)}, u32[]{:S(2)}) %collective-permute-start.25) | collective-permute-done | bytes 720928 | tf_op jit(solution)/shard_map/ppermute | solution.py:527
  419.3 16.5 %collective-permute-done.28 = bf16[352,1024]{1,0:T(8,128)(2,1)S(1)} collective-permute-done((bf16[352,1024]{1,0:T(8,128)(2,1)S(1)}, bf16[352,1024]{1,0:T(8,128)(2,1)S(1)}, u32[]{:S(2)}, u32[]{:S(2)}) %collective-permute-start.28) | collective-permute-done | bytes 720928 | tf_op jit(solution)/shard_map/ppermute | solution.py:532
  444.6 14.7 %collective-permute-done.29 = bf16[128,1024]{1,0:T(8,128)(2,1)S(1)} collective-permute-done((bf16[128,1024]{1,0:T(8,128)(2,1)S(1)}, bf16[128,1024]{1,0:T(8,128)(2,1)S(1)}, u32[]{:S(2)}, u32[]{:S(2)}) %collective-permute-start.29) | collective-permute-done | bytes 262176 | tf_op jit(solution)/shard_map/ppermute | solution.py:527
  478.7 17.4 %collective-permute-done.33.refs_3_ = bf16[128,1024]{1,0:T(8,128)(2,1)S(1)} collective-permute-done((bf16[128,1024]{1,0:T(8,128)(2,1)S(1)}, bf16[128,1024]{1,0:T(8,128)(2,1)S(1)}, u32[]{:S(2)}, u32[]{:S(2)}) %collective-permute-start.33) | collective-permute-done | bytes 262176 | tf_op jit(solution)/shard_map/ppermute | solution.py:527
  504.4 37.1 %newton.2 = (bf16[352,1024]{1,0:T(8,128)(2,1)}, bf16[352,1024]{1,0:T(8,128)(2,1)}) custom-call(bf16[1056,1024]{1,0:T(8,128)(2,1)} %constant_dynamic-update-slice_fusion.refs_0_, bf16[1056,1024]{1,0:T(8,128)(2,1)} %collective-permute-done.38.refs_1_, bf16[352,1024]{1,0:T(8,128)(2,1)} %copy-done.43, bf16[352,1024]{1,0:T(8,128)(2,1)} %copy-done.44, ...), custom_call_target="tpu_custom_call" | custom-call | flops 412048424960 | bytes 86507520 | tf_op jit(solution)/shard_map/newton/pallas_call | solution.py:481
  545.5 27.3 %newton.3 = (bf16[128,1024]{1,0:T(8,128)(2,1)}, bf16[128,1024]{1,0:T(8,128)(2,1)}) custom-call(bf16[1024,1024]{1,0:T(8,128)(2,1)} %all-gather.10.cloned.1.call-done.refs_0_, bf16[256,1024]{1,0:T(8,128)(2,1)} %pad_maximum_fusion.9.refs_1_), custom_call_target="tpu_custom_call" | custom-call | flops 327491256320 | bytes 31457280 | tf_op jit(solution)/shard_map/newton/pallas_call | solution.py:481
  572.9 19.9 %collective-permute-done.34.refs_4_ = bf16[480,1024]{1,0:T(8,128)(2,1)} collective-permute-done((bf16[480,1024]{1,0:T(8,128)(2,1)}, bf16[480,1024]{1,0:T(8,128)(2,1)}, u32[]{:S(2)}, u32[]{:S(2)}) %collective-permute-start.34) | collective-permute-done | bytes 983072 | tf_op jit(solution)/shard_map/ppermute | solution.py:527
  597.1 11.2 %collective-permute-done.45.refs_3_ = bf16[352,1024]{1,0:T(8,128)(2,1)} collective-permute-done((bf16[352,1024]{1,0:T(8,128)(2,1)}, bf16[352,1024]{1,0:T(8,128)(2,1)}, u32[]{:S(2)}, u32[]{:S(2)}) %collective-permute-start.45) | collective-permute-done | bytes 720928 | tf_op jit(solution)/shard_map/ppermute | solution.py:527
  608.3 15.4 %collective-permute-done.46.refs_4_ = bf16[352,1024]{1,0:T(8,128)(2,1)} collective-permute-done((bf16[352,1024]{1,0:T(8,128)(2,1)}, bf16[352,1024]{1,0:T(8,128)(2,1)}, u32[]{:S(2)}, u32[]{:S(2)}) %collective-permute-start.46) | collective-permute-done | bytes 720928 | tf_op jit(solution)/shard_map/ppermute | solution.py:527
  641.2 11.4 %collective-permute-done.48.refs_4_ = bf16[128,1024]{1,0:T(8,128)(2,1)S(1)} collective-permute-done((bf16[128,1024]{1,0:T(8,128)(2,1)S(1)}, bf16[128,1024]{1,0:T(8,128)(2,1)S(1)}, u32[]{:S(2)}, u32[]{:S(2)}) %collective-permute-start.48) | collective-permute-done | bytes 262176 | tf_op jit(solution)/shard_map/ppermute | solution.py:527
  679.4 13.8 %collective-permute-done.51.refs_6_ = bf16[704,1024]{1,0:T(8,128)(2,1)S(1)} collective-permute-done((bf16[704,1024]{1,0:T(8,128)(2,1)}, bf16[704,1024]{1,0:T(8,128)(2,1)S(1)}, u32[]{:S(2)}, u32[]{:S(2)}) %collective-permute-start.51) | collective-permute-done | bytes 1441824 | tf_op jit(solution)/shard_map/ppermute | solution.py:527
  (274 shorter events, 281.8 us)
Async XLA Ops:
  10.8 72.4 %all-gather.8.cloned.1.call-start = ((), (), s32[]{:S(2)}) async-start(), calls=%async_computation.3 | async-start | bytes 5242880 | tf_op jit(solution)/shard_map/all_gather | solution.py:785
  12.0 109.3 %all-gather.12.cloned.1.call-start = ((), (), s32[]{:S(2)}) async-start(), calls=%async_computation.7 | async-start | bytes 2621440 | tf_op jit(solution)/shard_map/all_gather | solution.py:785
  22.0 275.2 %reduce-scatter.3.cloned.1.call-start = ((), (), s32[]{:S(2)}) async-start(), calls=%async_computation.4 | async-start | bytes 2621440 | tf_op jit(solution)/shard_map/reduce_scatter | solution.py:944
  60.7 45.6 %collective-permute-start.5 = (bf16[4,8,64,128]{3,2,1,0:T(8,128)(2,1)}, bf16[4,8,64,128]{3,2,1,0:T(8,128)(2,1)S(1)}, u32[]{:S(2)}, u32[]{:S(2)}) collective-permute-start(bf16[4,8,64,128]{3,2,1,0:T(8,128)(2,1)} %get-tuple-element.175), channel_id=1, source_target_pairs={{0,16},{4,20},{8,24},{12,28},{1,17},{5,21},{9,25},{13,29},{2,18},{... | collective-permute-start | bytes 1572872 | tf_op jit(solution)/shard_map/ppermute | solution.py:527
  65.2 89.5 %collective-permute-start.11 = (bf16[1024,1024]{1,0:T(8,128)(2,1)}, bf16[1024,1024]{1,0:T(8,128)(2,1)}, u32[]{:S(2)}, u32[]{:S(2)}) collective-permute-start(bf16[1024,1024]{1,0:T(8,128)(2,1)} %bitcast.21.refs_2_.refs_4_.cot_ref), channel_id=1, source_target_pairs={{0,1},{1,0},{2,3},{3,2},{4,5},{5,4},{6,7},{7,6},{8,9},{9,8},{10,11... | collective-permute-start | bytes 6291464 | tf_op jit(solution)/shard_map/ppermute | solution.py:532
  83.3 49.8 %collective-permute-start.12 = (bf16[1,352,1024]{2,1,0:T(8,128)(2,1)}, bf16[1,352,1024]{2,1,0:T(8,128)(2,1)}, u32[]{:S(2)}, u32[]{:S(2)}) collective-permute-start(bf16[1,352,1024]{2,1,0:T(8,128)(2,1)} %dynamic-slice_bitcast_fusion.9), channel_id=1, source_target_pairs={{0,2},{1,3},{2,0},{3,1},{4,6},{5,7},{6,4},{7,5},{8,10},{9,11},{10,... | collective-permute-start | bytes 2162696 | tf_op jit(solution)/shard_map/ppermute | solution.py:532
  174.8 87.0 %collective-permute-start.14 = (bf16[3,352,1024]{2,1,0:T(8,128)(2,1)}, bf16[3,352,1024]{2,1,0:T(8,128)(2,1)}, u32[]{:S(2)}, u32[]{:S(2)}) collective-permute-start(bf16[3,352,1024]{2,1,0:T(8,128)(2,1)} %get-tuple-element.198), channel_id=1, source_target_pairs={{0,4},{4,0},{8,12},{12,8},{16,20},{20,16},{24,28},{28,24},{1,5},{5... | collective-permute-start | bytes 6488072 | tf_op jit(solution)/shard_map/ppermute | solution.py:527
  229.0 55.7 %collective-permute-start.15 = (bf16[3,352,1024]{2,1,0:T(8,128)(2,1)}, bf16[3,352,1024]{2,1,0:T(8,128)(2,1)}, u32[]{:S(2)}, u32[]{:S(2)}) collective-permute-start(bf16[3,352,1024]{2,1,0:T(8,128)(2,1)} %get-tuple-element.209), channel_id=1, source_target_pairs={{0,4},{4,0},{8,12},{12,8},{16,20},{20,16},{24,28},{28,24},{1,5},{5... | collective-permute-start | bytes 6488072 | tf_op jit(solution)/shard_map/ppermute | solution.py:527
  261.8 149.7 %reduce-scatter.5.cloned.1.call-start = ((), (), s32[]{:S(2)}) async-start(), calls=%async_computation.5 | async-start | bytes 10485760 | tf_op jit(solution)/shard_map/reduce_scatter | solution.py:944
  287.4 52.1 %collective-permute-start.17 = (bf16[3,352,1024]{2,1,0:T(8,128)(2,1)S(1)}, bf16[3,352,1024]{2,1,0:T(8,128)(2,1)}, u32[]{:S(2)}, u32[]{:S(2)}) collective-permute-start(bf16[3,352,1024]{2,1,0:T(8,128)(2,1)S(1)} %add_convert_fusion.1), channel_id=1, source_target_pairs={{0,2},{1,3},{2,0},{3,1},{4,6},{5,7},{6,4},{7,5},{8,10},{9,11},{10,... | collective-permute-start | bytes 6488072 | tf_op jit(solution)/shard_map/ppermute | solution.py:532
  339.6 202.0 %all-gather.10.cloned.1.call-start = ((), (), s32[]{:S(2)}) async-start(), calls=%async_computation.6 | async-start | bytes 2621440 | tf_op jit(solution)/shard_map/all_gather | solution.py:1045
  345.9 49.0 %collective-permute-start.24 = (bf16[352,1024]{1,0:T(8,128)(2,1)S(1)}, bf16[352,1024]{1,0:T(8,128)(2,1)S(1)}, u32[]{:S(2)}, u32[]{:S(2)}) collective-permute-start(bf16[352,1024]{1,0:T(8,128)(2,1)S(1)} %get-tuple-element.329), channel_id=1, source_target_pairs={{0,8},{4,12},{8,16},{12,20},{16,24},{20,28},{24,0},{28,4},{1,9},{5... | collective-permute-start | bytes 2162696 | tf_op jit(solution)/shard_map/ppermute | solution.py:527
  347.4 61.8 %collective-permute-start.25 = (bf16[352,1024]{1,0:T(8,128)(2,1)S(1)}, bf16[352,1024]{1,0:T(8,128)(2,1)S(1)}, u32[]{:S(2)}, u32[]{:S(2)}) collective-permute-start(bf16[352,1024]{1,0:T(8,128)(2,1)S(1)} %get-tuple-element.328), channel_id=1, source_target_pairs={{0,16},{4,20},{8,24},{12,28},{16,0},{20,4},{24,8},{28,12},{1,17},{... | collective-permute-start | bytes 2162696 | tf_op jit(solution)/shard_map/ppermute | solution.py:527
  348.9 62.4 %collective-permute-start.26 = (bf16[352,1024]{1,0:T(8,128)(2,1)S(1)}, bf16[352,1024]{1,0:T(8,128)(2,1)}, u32[]{:S(2)}, u32[]{:S(2)}) collective-permute-start(bf16[352,1024]{1,0:T(8,128)(2,1)S(1)} %get-tuple-element.327), channel_id=1, source_target_pairs={{0,24},{4,28},{8,0},{12,4},{16,8},{20,12},{24,16},{28,20},{1,25},{... | collective-permute-start | bytes 2162696 | tf_op jit(solution)/shard_map/ppermute | solution.py:527
  418.7 45.6 %collective-permute-start.36 = (bf16[352,1024]{1,0:T(8,128)(2,1)S(1)}, bf16[352,1024]{1,0:T(8,128)(2,1)S(1)}, u32[]{:S(2)}, u32[]{:S(2)}) collective-permute-start(bf16[352,1024]{1,0:T(8,128)(2,1)S(1)} %get-tuple-element.258), channel_id=1, source_target_pairs={{0,4},{4,0},{8,12},{12,8},{16,20},{20,16},{24,28},{28,24},{1,5},{5... | collective-permute-start | bytes 2162696 | tf_op jit(solution)/shard_map/ppermute | solution.py:527
  496.1 96.8 %collective-permute-start.34 = (bf16[480,1024]{1,0:T(8,128)(2,1)}, bf16[480,1024]{1,0:T(8,128)(2,1)}, u32[]{:S(2)}, u32[]{:S(2)}) collective-permute-start(bf16[480,1024]{1,0:T(8,128)(2,1)} %pad_maximum_fusion.7), channel_id=1, source_target_pairs={{0,16},{4,20},{8,24},{12,28},{16,0},{20,4},{24,8},{28,12},{1,17},{... | collective-permute-start | bytes 2949128 | tf_op jit(solution)/shard_map/ppermute | solution.py:527
  498.5 95.4 %collective-permute-start.35 = (bf16[480,1024]{1,0:T(8,128)(2,1)}, bf16[480,1024]{1,0:T(8,128)(2,1)}, u32[]{:S(2)}, u32[]{:S(2)}) collective-permute-start(bf16[480,1024]{1,0:T(8,128)(2,1)} %pad_maximum_fusion.7), channel_id=1, source_target_pairs={{0,24},{4,28},{8,0},{12,4},{16,8},{20,12},{24,16},{28,20},{1,25},{... | collective-permute-start | bytes 2949128 | tf_op jit(solution)/shard_map/ppermute | solution.py:527
  502.1 43.4 %collective-permute-start.41 = (bf16[704,1024]{1,0:T(8,128)(2,1)}, bf16[704,1024]{1,0:T(8,128)(2,1)}, u32[]{:S(2)}, u32[]{:S(2)}) collective-permute-start(bf16[704,1024]{1,0:T(8,128)(2,1)} %constant_dynamic-update-slice_fusion.3), channel_id=1, source_target_pairs={{0,4},{4,0},{8,12},{12,8},{16,20},{20,16},{24,28},{28,24},{1,5},{5... | collective-permute-start | bytes 4325384 | tf_op jit(solution)/shard_map/ppermute | solution.py:527
  541.6 66.7 %collective-permute-start.45 = (bf16[352,1024]{1,0:T(8,128)(2,1)}, bf16[352,1024]{1,0:T(8,128)(2,1)}, u32[]{:S(2)}, u32[]{:S(2)}) collective-permute-start(bf16[352,1024]{1,0:T(8,128)(2,1)} %get-tuple-element.299.refs_1_), channel_id=1, source_target_pairs={{0,8},{4,12},{8,16},{12,20},{16,24},{20,28},{24,0},{28,4},{1,9},{5... | collective-permute-start | bytes 2162696 | tf_op jit(solution)/shard_map/ppermute | solution.py:527
  542.9 80.7 %collective-permute-start.46 = (bf16[352,1024]{1,0:T(8,128)(2,1)}, bf16[352,1024]{1,0:T(8,128)(2,1)}, u32[]{:S(2)}, u32[]{:S(2)}) collective-permute-start(bf16[352,1024]{1,0:T(8,128)(2,1)} %get-tuple-element.299.refs_1_), channel_id=1, source_target_pairs={{0,16},{4,20},{8,24},{12,28},{16,0},{20,4},{24,8},{28,12},{1,17},{... | collective-permute-start | bytes 2162696 | tf_op jit(solution)/shard_map/ppermute | solution.py:527
  572.8 51.7 %collective-permute-start.43 = (bf16[352,1024]{1,0:T(8,128)(2,1)S(1)}, bf16[352,1024]{1,0:T(8,128)(2,1)S(1)}, u32[]{:S(2)}, u32[]{:S(2)}) collective-permute-start(bf16[352,1024]{1,0:T(8,128)(2,1)S(1)} %copy-done.26), channel_id=1, source_target_pairs={{0,24},{4,28},{8,0},{12,4},{16,8},{20,12},{24,16},{28,20},{1,25},{... | collective-permute-start | bytes 2162696 | tf_op jit(solution)/shard_map/ppermute | solution.py:527
  595.5 68.4 %collective-permute-start.42 = (bf16[1088,1024]{1,0:T(8,128)(2,1)S(1)}, bf16[1088,1024]{1,0:T(8,128)(2,1)S(1)}, u32[]{:S(2)}, u32[]{:S(2)}) collective-permute-start(bf16[1088,1024]{1,0:T(8,128)(2,1)S(1)} %pad_maximum_fusion.1), channel_id=1, source_target_pairs={{0,4},{4,0},{8,12},{12,8},{16,20},{20,16},{24,28},{28,24},{1,5},{5... | collective-permute-start | bytes 6684680 | tf_op jit(solution)/shard_map/ppermute | solution.py:527
  630.0 63.2 %collective-permute-start.51 = (bf16[704,1024]{1,0:T(8,128)(2,1)}, bf16[704,1024]{1,0:T(8,128)(2,1)S(1)}, u32[]{:S(2)}, u32[]{:S(2)}) collective-permute-start(bf16[704,1024]{1,0:T(8,128)(2,1)} %constant_dynamic-update-slice_fusion.5), channel_id=1, source_target_pairs={{0,4},{4,0},{8,12},{12,8},{16,20},{20,16},{24,28},{28,24},{1,5},{5... | collective-permute-start | bytes 4325384 | tf_op jit(solution)/shard_map/ppermute | solution.py:527
  662.4 46.6 %collective-permute-start.50 = (bf16[384,1024]{1,0:T(8,128)(2,1)S(1)}, bf16[384,1024]{1,0:T(8,128)(2,1)S(1)}, u32[]{:S(2)}, u32[]{:S(2)}) collective-permute-start(bf16[384,1024]{1,0:T(8,128)(2,1)S(1)} %pad_maximum_fusion.8), channel_id=1, source_target_pairs={{0,4},{4,0},{8,12},{12,8},{16,20},{20,16},{24,28},{28,24},{1,5},{5... | collective-permute-start | bytes 2359304 | tf_op jit(solution)/shard_map/ppermute | solution.py:527
  (81 other events, 1474.0 us)
Sparse Core Ops, SparseCore 0:
  10.9 35.6 all-gather.5
  48.7 34.4 all-gather.7
  84.8 30.0 all-gather.11
  261.9 35.2 reduce-scatter.2
  339.7 71.6 reduce-scatter.4
  500.3 22.2 all-gather.9

commit v2 on v1

--- a/solution.py
+++ b/solution.py
@@ -1052,8 +1052,7 @@
         mix_all.add(part, (own, 0, j))
     both = jnp.concatenate([wide_grad, mix_grad], axis=0)
     mix_first = places.send(tied(mix_grad, mix_low), "quads", 1)
-    both = tied(both, (mix_low, mix_first))
-    second, third = (places.send(both, "quads", k) for k in (2, 3))
+    second = places.send(tied(both, (mix_low, mix_first)), "quads", 2)
     early = jnp.concatenate(tied([wide_grad, wide_first], mix_known), axis=0)
     early_arrived = to_members(early)
     for j, part in enumerate(early_arrived, 1):
@@ -1063,31 +1062,36 @@
     wide_x, mix_x = Blocks(places, rows), Blocks(places, own)
     wide_x.add(wide_rows, (0, 0, 0))
     wide_x.add(wide_rest, *[((j - 1) * rows, 0, j) for j in range(1, places.members)])
+    second, mix_first = tied((second, mix_first), wide_rows)
+    nearer = jnp.concatenate([second, mix_first], axis=0)
+    nearer_arrived = to_members(nearer)
+    wide_all.add(second, (0, 2, 0))
+    mix_all.add(second, (rows, 2, 0))
+    mix_all.add(mix_first, (0, 1, 0))
+    for j, part in enumerate(nearer_arrived, 1):
+        wide_all.add(part, (0, 2, j))
+        mix_all.add(part, (rows, 2, j), (rows + own, 1, j))
     x_sent = tied(wide_rows, mix_every)
     x_parts = [places.send(x_sent, "quads", k) for k in (1, 2)]
-    mix_rows, mix_rest = newton_rows([tied(mix_every, (wide_rows, early_arrived))], mix_known, own)
-    later = jnp.concatenate(tied([second, third, mix_first], mix_rows), axis=0)
-    wide_all.add(second, (0, 2, 0))
-    wide_all.add(third, (0, 3, 0))
-    mix_all.add(mix_first, (0, 1, 0))
-    mix_all.add(second, (rows, 2, 0))
-    mix_all.add(third, (rows, 3, 0))
-    for j, part in enumerate(to_members(later), 1):
-        step = rows + own
-        wide_all.add(part, (0, 2, j), (step, 3, j))
-        mix_all.add(part, (2 * step, 1, j), (rows, 2, j), (step + rows, 3, j))
-    x_parts.append(places.send(tied(x_sent, mix_rows), "quads", 3))
+    mix_rows, mix_rest = newton_rows([tied(mix_every, (wide_rows, early_arrived, nearer))], mix_known, own)
+    x_pair = jnp.concatenate(tied(x_parts, (mix_rows, nearer_arrived)), axis=0)
+    third = places.send(tied(both, x_pair), "quads", 3)
+    x_parts.append(places.send(tied(x_sent, x_pair), "quads", 3))
     for k, part in enumerate(x_parts, 1):
         wide_x.add(part, (0, k, 0))
-    x_pair = jnp.concatenate(tied(x_parts[:2], mix_rows), axis=0)
     x_arrived = to_members(x_pair)
     for j, part in enumerate(x_arrived, 1):
         wide_x.add(part, (0, 1, j), (rows, 2, j))
+    wide_all.add(third, (0, 3, 0))
+    mix_all.add(third, (rows, 3, 0))
+    for j, part in enumerate(to_members(third), 1):
+        wide_all.add(part, (0, 3, j))
+        mix_all.add(part, (rows, 3, j))
     mix_x.add(mix_rows, (0, 0, 0))
     mix_x.add(mix_rest, *[((j - 1) * own, 0, j) for j in range(1, places.members)])
-    mix_sent = tied(mix_rows, (x_pair, x_parts[2]))
+    mix_sent = tied(mix_rows, x_arrived)
     mix_parts = [places.send(mix_sent, "quads", k) for k in (1, 2, 3)]
-    x_last = to_members(x_parts[2])
+    x_last = to_members(tied(x_parts[2], third))
     for j, part in enumerate(x_last, 1):
         wide_x.add(part, (0, 3, j))
     for k, part in enumerate(mix_parts, 1):
@@ -1099,16 +1103,16 @@
     wide_groups = [(0, None, hidden_rows), (1, 0, hidden_rows), (1, 1, hidden_rows), (2, None, width_rows)]
     mix_groups = [(0, i, width_rows) for i in range(4)]
     ones = [1.0] * 4
-    mom_down, mom_in, mom_out = wide_all.finished(
-        (m_down, m_in, m_out), wide_groups, (MOMENTUM, ones), late=x_last
-    )
-    (mom_mix,) = mix_all.finished((m_mix,), mix_groups, (MOMENTUM, ones), late=x_last)
     factor = math.sqrt(FF / D)
     steps = [-STEP_RATE, -STEP_RATE * factor, -STEP_RATE * factor, -STEP_RATE]
     new_down, new_in, new_out, copy_down, copy_in, copy_out = wide_x.finished(
-        (w_down, w_in, w_out), wide_groups, (1.0, steps), True, late=(mom_down, mom_in, mom_out, mom_mix)
+        (w_down, w_in, w_out), wide_groups, (1.0, steps), True
     )
-    new_mix, copy_mix = mix_x.finished((w_mix,), mix_groups, (1.0, [-STEP_RATE] * 4), True, late=new_in)
+    mom_down, mom_in, mom_out = wide_all.finished(
+        (m_down, m_in, m_out), wide_groups, (MOMENTUM, ones), late=new_in
+    )
+    (mom_mix,) = mix_all.finished((m_mix,), mix_groups, (MOMENTUM, ones), late=mom_in)
+    new_mix, copy_mix = mix_x.finished((w_mix,), mix_groups, (1.0, [-STEP_RATE] * 4), True, late=mom_mix)
     return (
         activations.reshape(tokens.shape),
         input_grad,

time: 728 us -> 714 us (0.981)
  waiting for transfers between devices: 279 us -> 258 us
    ppermute x40 -> x41, waiting for transfers between devices: 207 us -> 186 us  [send(): return lax.ppermute(value, 'seq', pairs)]
    ppermute x40 -> x41, starting transfers between devices: 60.5 us -> 65.9 us  [send(): return lax.ppermute(value, 'seq', pairs)]
    unnamed x98 -> x101, local copies, waits for them, and re-layouts: 15.4 us -> 16.1 us
  transfers between devices with their start and end apart: 58 -> 59, of which waited for: 33 -> 28; matrix products, arithmetic and copies ran while one was open for 6% -> 6% of each run, Pallas kernels for 41% -> 42%
where the time goes in v2:
time: 714 us; the launch traced here: 705 us
  Pallas kernels  299 us (42%)
  waiting for transfers between devices  258 us (36%)
  starting transfers between devices  71.3 us (10%)
  other arithmetic  31.9 us (4%)
  local copies, waits for them, and re-layouts  30.3 us (4%)
  between operations  15.2 us (2%)
    ppermute x41, waiting for transfers between devices, send(): return lax.ppermute(value, 'seq', pairs)  186 us
    pallas_call x4, Pallas kernels, ffn(): pl.pallas_call(body, in_specs=[pl.BlockSpec(memory_space=pltpu.SMEM)] * l...  79.2 us
    ppermute x41, starting transfers between devices, send(): return lax.ppermute(value, 'seq', pairs)  65.9 us
    pallas_call x2, Pallas kernels, newton_rows(): pl.pallas_call(lambda *refs: newton_kernel(len(every), *refs), out_shape=...  64.5 us
    all_gather x3, waiting for transfers between devices, gathered(): lax.all_gather(jnp.stack(rows).astype(BF16), 'batch', axis=1, tiled=True)  30.1 us
    pallas_call x4, Pallas kernels, finished(): pl.pallas_call(lambda *refs: finish_kernel(places.members, self.sources,...  29.7 us
    ppermute x10, waiting for transfers between devices, send(): return lax.ppermute(value, 'batch', pairs)  24 us
    pallas_call x1, Pallas kernels, shards(): pl.pallas_call(lambda *refs: att_back_kernel(seqs, *refs), grid=(tiles,),...  22.8 us
  transfers between devices with their start and end apart: 59, of which 28 were waited for; matrix products, arithmetic and copies ran while one was open for 6% of the time, Pallas kernels for 42%

profile of v2, /device:TPU:8, one launch (start us, length us, event | category | flops | bytes accessed | tf_op | source)
XLA Modules:
  0.0 705.2 jit_solution(11241230767717955627)
XLA Ops:
  33.5 13.1 %all-gather.6.cloned.1.call-done.refs_1_.w_ref = bf16[2,1024,1024]{2,1,0:T(8,128)(2,1)} async-done(((bf16[2,256,1024]{2,1,0:T(8,128)(2,1)}), bf16[2,1024,1024]{2,1,0:T(8,128)(2,1)}) %all-gather.6.cloned.1.call-update) | async-done | bytes 4194320 | tf_op jit(solution)/shard_map/all_gather | solution.py:785
  46.6 10.7 %kv.1 = (bf16[1024,1024]{1,0:T(8,128)(2,1)}, bf16[1024,1024]{1,0:T(8,128)(2,1)}, bf16[1024,1024]{1,0:T(8,128)(2,1)}, bf16[1024,1024]{1,0:T(8,128)(2,1)}, bf16[4,8,64,128]{3,2,1,0:T(8,128)(2,1)}) custom-call(bf16[1024,1024]{1,0:T(8,128)(2,1)} %bitcast.139, bf16[2,1024,1024]{2,1,0:T(8,128)(2,1)} %all-gather.6.cloned.1.call-done.refs_1_.w_ref, ...), custom_call_target="tpu_custom_call" | custom-call | flops 42949672960 | bytes 167772160 | tf_op jit(solution)/shard_map/kv/pallas_call | solution.py:824
  66.2 17.0 %all-gather.8.cloned.1.call-done.refs_1_.w_ref = bf16[2,1024,1024]{2,1,0:T(8,128)(2,1)} async-done(((bf16[2,256,1024]{2,1,0:T(8,128)(2,1)}), bf16[2,1024,1024]{2,1,0:T(8,128)(2,1)}) %all-gather.8.cloned.1.call-update) | async-done | bytes 4194320 | tf_op jit(solution)/shard_map/all_gather | solution.py:785
  83.8 15.9 %query.1 = (bf16[1024,1024]{1,0:T(8,128)(2,1)}, bf16[1024,1024]{1,0:T(8,128)(2,1)}, bf16[1024,1024]{1,0:T(8,128)(2,1)}, f32[1024,1024]{1,0:T(8,128)}) custom-call(bf16[1024,1024]{1,0:T(8,128)(2,1)} %get-tuple-element.171.refs_0_.nf_ref.refs_9_.refs_7_, bf16[2,1024,1024]{2,1,0:T(8,128)(2,1)} %all-gather.8.cloned.1.call-done.refs_1_.w_ref, ...), custom_call_target="tpu_custom_call" | custom-call | flops 85899345920 | bytes 167772160 | tf_op jit(solution)/shard_map/query/pallas_call | solution.py:842
  121.3 11.6 %middle.1 = (f32[1024,1024]{1,0:T(8,128)}, bf16[1024,1024]{1,0:T(8,128)(2,1)}, f32[1024,1024]{1,0:T(8,128)}, bf16[1024,1024]{1,0:T(8,128)(2,1)}) custom-call(f32[1024,1024]{1,0:T(8,128)} %get-tuple-element.175.o_ref, bf16[1024,1024]{1,0:T(8,128)(2,1)} %get-tuple-element.176.q_ref.refs_0_, bf16[4,8,64,128]{3,2,1,0:T(8,128)(2,1)} %add_convert_fusion.7.state_ref.refs_7_, ...), custom_call_target="tpu_custom_call" | custom-call | flops 21474836480 | bytes 251658240 | tf_op jit(solution)/shard_map/middle/pallas_call | solution.py:853
  133.1 19.5 %ffn.4 = (f32[1024,1024]{1,0:T(8,128)}, f32[1024,1024]{1,0:T(8,128)}, bf16[3,704,1024]{2,1,0:T(8,128)(2,1)}) custom-call(bf16[1024,1024]{1,0:T(8,128)(2,1)} %get-tuple-element.181.refs_0_.refs_1_, bf16[2,704,1024]{2,1,0:T(8,128)(2,1)} %copy-done.4, bf16[1024,1024]{1,0:T(8,128)(2,1)} %bitcast.21.refs_2_.refs_4_.cot_ref, ...), custom_call_target="tpu_custom_call" | custom-call | flops 118111600640 | bytes 212336640 | tf_op jit(solution)/shard_map/ffn/pallas_call | solution.py:317
  156.0 18.8 %ffn.5 = (f32[1024,1024]{1,0:T(8,128)}, f32[1024,1024]{1,0:T(8,128)}, bf16[3,352,1024]{2,1,0:T(8,128)(2,1)}, bf16[3,352,1024]{2,1,0:T(8,128)(2,1)}) custom-call(bf16[1024,1024]{1,0:T(8,128)(2,1)} %copy-done.41, bf16[2,704,1024]{2,1,0:T(8,128)(2,1)} %copy-done.4, bf16[1024,1024]{1,0:T(8,128)(2,1)} %collective-permute-done.11.refs_2_.refs_4_, ...), custom_call_target="tpu_custom_call" | custom-call | flops 118111600640 | bytes 212336640 | tf_op jit(solution)/shard_map/ffn/pallas_call | solution.py:317
  176.3 10.5 %collective-permute-done.9.refs_3_ = bf16[2,352,1024]{2,1,0:T(8,128)(2,1)S(1)} collective-permute-done((bf16[2,352,1024]{2,1,0:T(8,128)(2,1)}, bf16[2,352,1024]{2,1,0:T(8,128)(2,1)S(1)}, u32[]{:S(2)}, u32[]{:S(2)}) %collective-permute-start.9) | collective-permute-done | bytes 1441824 | tf_op jit(solution)/shard_map/ppermute | solution.py:539
  187.9 19.7 %ffn.6 = (bf16[1024,1024]{1,0:T(8,128)(2,1)}, bf16[1024,1024]{1,0:T(8,128)(2,1)}, bf16[3,704,1024]{2,1,0:T(8,128)(2,1)}) custom-call(s32[1]{0:T(128)} %bitcast.refs_0_, bf16[1024,1024]{1,0:T(8,128)(2,1)} %copy-done.41, bf16[2,352,1024]{2,1,0:T(8,128)(2,1)} %collective-permute-done.8.refs_2_, bf16[2,352,1024]{2,1,0:T(8,128)(2,1)} %copy-done.43, ...), custom_call_target="tpu_custom_call" | custom-call | flops 118111600640 | bytes 212336640 | tf_op jit(solution)/shard_map/ffn/pallas_call | solution.py:317
  207.7 21.2 %ffn.7 = (f32[1024,1024]{1,0:T(8,128)}, f32[1024,1024]{1,0:T(8,128)}, bf16[3,352,1024]{2,1,0:T(8,128)(2,1)}, bf16[3,352,1024]{2,1,0:T(8,128)(2,1)}) custom-call(s32[1]{0:T(128)} %bitcast.refs_0_, bf16[1024,1024]{1,0:T(8,128)(2,1)} %get-tuple-element.181.refs_0_.refs_1_, bf16[2,352,1024]{2,1,0:T(8,128)(2,1)} %collective-permute-done.8.refs_2_, ...), custom_call_target="tpu_custom_call" | custom-call | flops 118111600640 | bytes 212336640 | tf_op jit(solution)/shard_map/ffn/pallas_call | solution.py:317
  231.8 14.1 %gate_back.1 = (bf16[1024,1024]{1,0:T(8,128)(2,1)}, bf16[1024,1024]{1,0:T(8,128)(2,1)}, bf16[1024,1024]{1,0:T(8,128)(2,1)}, bf16[4,8,64,128]{3,2,1,0:T(8,128)(2,1)}) custom-call(f32[1024,1024]{1,0:T(8,128)} %get-tuple-element.213.dn_ref, bf16[1024,1024]{1,0:T(8,128)(2,1)} %copy-done.42, f32[1024,1024]{1,0:T(8,128)} %get-tuple-element.185.refs_4_.mid_ref, ...), custom_call_target="tpu_custom_call" | custom-call | flops 21474836480 | bytes 167772160 | tf_op jit(solution)/shard_map/gate_back/pallas_call | solution.py:896
  261.9 22.8 %attention_back.1 = (bf16[1024,1024]{1,0:T(8,128)(2,1)}, f32[1024,1024]{1,0:T(8,128)}, f32[1024,1024]{1,0:T(8,128)}, bf16[4,1024,1024]{2,1,0:T(8,128)(2,1)}) custom-call(bf16[1024,1024]{1,0:T(8,128)(2,1)} %get-tuple-element.176.q_ref.refs_0_, bf16[1024,1024]{1,0:T(8,128)(2,1)} %get-tuple-element.172.refs_2_.refs_1_.refs_0_, ...), custom_call_target="tpu_custom_call", output_to_operand_aliasing={{3}: (10, {})} | custom-call | flops 85899345920 | bytes 209715200 | tf_op jit(solution)/shard_map/attention_back/pallas_call | solution.py:930
  319.4 12.7 %state_back.1 = (bf16[2,1024,1024]{2,1,0:T(8,128)(2,1)}, bf16[4,1024,1024]{2,1,0:T(8,128)(2,1)}) custom-call(bf16[1024,1024]{1,0:T(8,128)(2,1)} %get-tuple-element.172.refs_2_.refs_1_.refs_0_, bf16[1024,1024]{1,0:T(8,128)(2,1)} %get-tuple-element.173.refs_3_.refs_2_.refs_1_, ...), custom_call_target="tpu_custom_call", output_to_operand_aliasing={{1}: (8, {})} | custom-call | flops 53687091200 | bytes 188743680 | tf_op jit(solution)/shard_map/state_back/pallas_call | solution.py:971
  354.8 11.0 %input_back.1 = bf16[1024,1024]{1,0:T(8,128)(2,1)} custom-call(bf16[2,1024,1024]{2,1,0:T(8,128)(2,1)} %get-tuple-element.240.dkv_ref, bf16[2,1024,1024]{2,1,0:T(8,128)(2,1)} %all-gather.6.cloned.1.call-done.refs_1_.w_ref, f32[1024,1024]{1,0:T(8,128)} %normed_back.1.part_ref, bf16[1024,1024]{1,0:T(8,128)(2,1)} %bitcast.141, ...), custom_call_target="tpu_custom_call" | custom-call | flops 42949672960 | bytes 167772160 | tf_op jit(solution)/shard_map/input_back/pallas_call | solution.py:991
  365.7 29.2 %collective-permute-done.24 = bf16[352,1024]{1,0:T(8,128)(2,1)S(1)} collective-permute-done((bf16[352,1024]{1,0:T(8,128)(2,1)S(1)}, bf16[352,1024]{1,0:T(8,128)(2,1)S(1)}, u32[]{:S(2)}, u32[]{:S(2)}) %collective-permute-start.24) | collective-permute-done | bytes 720928 | tf_op jit(solution)/shard_map/ppermute | solution.py:527
  394.9 14.3 %collective-permute-done.25 = bf16[352,1024]{1,0:T(8,128)(2,1)S(1)} collective-permute-done((bf16[352,1024]{1,0:T(8,128)(2,1)S(1)}, bf16[352,1024]{1,0:T(8,128)(2,1)S(1)}, u32[]{:S(2)}, u32[]{:S(2)}) %collective-permute-start.25) | collective-permute-done | bytes 720928 | tf_op jit(solution)/shard_map/ppermute | solution.py:527
  419.0 16.5 %collective-permute-done.28 = bf16[352,1024]{1,0:T(8,128)(2,1)S(1)} collective-permute-done((bf16[352,1024]{1,0:T(8,128)(2,1)S(1)}, bf16[352,1024]{1,0:T(8,128)(2,1)S(1)}, u32[]{:S(2)}, u32[]{:S(2)}) %collective-permute-start.28) | collective-permute-done | bytes 720928 | tf_op jit(solution)/shard_map/ppermute | solution.py:532
  444.7 14.7 %collective-permute-done.29 = bf16[128,1024]{1,0:T(8,128)(2,1)S(1)} collective-permute-done((bf16[128,1024]{1,0:T(8,128)(2,1)S(1)}, bf16[128,1024]{1,0:T(8,128)(2,1)S(1)}, u32[]{:S(2)}, u32[]{:S(2)}) %collective-permute-start.29) | collective-permute-done | bytes 262176 | tf_op jit(solution)/shard_map/ppermute | solution.py:527
  478.8 17.4 %collective-permute-done.33.refs_4_ = bf16[128,1024]{1,0:T(8,128)(2,1)S(1)} collective-permute-done((bf16[128,1024]{1,0:T(8,128)(2,1)S(1)}, bf16[128,1024]{1,0:T(8,128)(2,1)S(1)}, u32[]{:S(2)}, u32[]{:S(2)}) %collective-permute-start.33) | collective-permute-done | bytes 262176 | tf_op jit(solution)/shard_map/ppermute | solution.py:527
  504.6 37.3 %newton.2 = (bf16[352,1024]{1,0:T(8,128)(2,1)}, bf16[352,1024]{1,0:T(8,128)(2,1)}) custom-call(bf16[1056,1024]{1,0:T(8,128)(2,1)} %constant_dynamic-update-slice_fusion.refs_0_, bf16[1056,1024]{1,0:T(8,128)(2,1)} %collective-permute-done.37.refs_1_, bf16[352,1024]{1,0:T(8,128)(2,1)} %copy-done.44, bf16[352,1024]{1,0:T(8,128)(2,1)} %copy-done.45, ...), custom_call_target="tpu_custom_call" | custom-call | flops 412048424960 | bytes 86507520 | tf_op jit(solution)/shard_map/newton/pallas_call | solution.py:481
  550.1 27.2 %newton.3 = (bf16[128,1024]{1,0:T(8,128)(2,1)}, bf16[128,1024]{1,0:T(8,128)(2,1)}) custom-call(bf16[1024,1024]{1,0:T(8,128)(2,1)} %all-gather.10.cloned.1.call-done.refs_0_, bf16[256,1024]{1,0:T(8,128)(2,1)} %pad_maximum_fusion.8.refs_1_), custom_call_target="tpu_custom_call" | custom-call | flops 327491256320 | bytes 31457280 | tf_op jit(solution)/shard_map/newton/pallas_call | solution.py:481
  577.4 15.0 %collective-permute-done.42.refs_4_ = bf16[352,1024]{1,0:T(8,128)(2,1)} collective-permute-done((bf16[352,1024]{1,0:T(8,128)(2,1)}, bf16[352,1024]{1,0:T(8,128)(2,1)}, u32[]{:S(2)}, u32[]{:S(2)}) %collective-permute-start.42) | collective-permute-done | bytes 720928 | tf_op jit(solution)/shard_map/ppermute | solution.py:527
  600.9 35.5 %collective-permute-done.46.refs_5_ = bf16[352,1024]{1,0:T(8,128)(2,1)S(1)} collective-permute-done((bf16[352,1024]{1,0:T(8,128)(2,1)}, bf16[352,1024]{1,0:T(8,128)(2,1)S(1)}, u32[]{:S(2)}, u32[]{:S(2)}) %collective-permute-start.46) | collective-permute-done | bytes 720928 | tf_op jit(solution)/shard_map/ppermute | solution.py:527
  643.6 12.2 %collective-permute-done.49.refs_3_ = bf16[128,1024]{1,0:T(8,128)(2,1)S(1)} collective-permute-done((bf16[128,1024]{1,0:T(8,128)(2,1)S(1)}, bf16[128,1024]{1,0:T(8,128)(2,1)S(1)}, u32[]{:S(2)}, u32[]{:S(2)}) %collective-permute-start.49) | collective-permute-done | bytes 262176 | tf_op jit(solution)/shard_map/ppermute | solution.py:527
  (279 shorter events, 252.2 us)
Async XLA Ops:
  10.8 72.4 %all-gather.8.cloned.1.call-start = ((), (), s32[]{:S(2)}) async-start(), calls=%async_computation.3 | async-start | bytes 5242880 | tf_op jit(solution)/shard_map/all_gather | solution.py:785
  12.0 109.3 %all-gather.12.cloned.1.call-start = ((), (), s32[]{:S(2)}) async-start(), calls=%async_computation.7 | async-start | bytes 2621440 | tf_op jit(solution)/shard_map/all_gather | solution.py:785
  22.0 275.2 %reduce-scatter.3.cloned.1.call-start = ((), (), s32[]{:S(2)}) async-start(), calls=%async_computation.4 | async-start | bytes 2621440 | tf_op jit(solution)/shard_map/reduce_scatter | solution.py:944
  57.3 42.5 %collective-permute-start.4 = (bf16[4,8,64,128]{3,2,1,0:T(8,128)(2,1)}, bf16[4,8,64,128]{3,2,1,0:T(8,128)(2,1)S(1)}, u32[]{:S(2)}, u32[]{:S(2)}) collective-permute-start(bf16[4,8,64,128]{3,2,1,0:T(8,128)(2,1)} %get-tuple-element.178), channel_id=1, source_target_pairs={{0,8},{4,12},{8,16},{12,20},{16,24},{20,28},{1,9},{5,13},{9,17},{1... | collective-permute-start | bytes 1572872 | tf_op jit(solution)/shard_map/ppermute | solution.py:527
  60.7 45.6 %collective-permute-start.5 = (bf16[4,8,64,128]{3,2,1,0:T(8,128)(2,1)}, bf16[4,8,64,128]{3,2,1,0:T(8,128)(2,1)S(1)}, u32[]{:S(2)}, u32[]{:S(2)}) collective-permute-start(bf16[4,8,64,128]{3,2,1,0:T(8,128)(2,1)} %get-tuple-element.178), channel_id=1, source_target_pairs={{0,16},{4,20},{8,24},{12,28},{1,17},{5,21},{9,25},{13,29},{2,18},{... | collective-permute-start | bytes 1572872 | tf_op jit(solution)/shard_map/ppermute | solution.py:527
  62.9 43.3 %collective-permute-start.6 = (bf16[4,8,64,128]{3,2,1,0:T(8,128)(2,1)}, bf16[4,8,64,128]{3,2,1,0:T(8,128)(2,1)S(1)}, u32[]{:S(2)}, u32[]{:S(2)}) collective-permute-start(bf16[4,8,64,128]{3,2,1,0:T(8,128)(2,1)} %get-tuple-element.178), channel_id=1, source_target_pairs={{0,24},{4,28},{1,25},{5,29},{2,26},{6,30},{3,27},{7,31}} | collective-permute-start | bytes 1572872 | tf_op jit(solution)/shard_map/ppermute | solution.py:527
  65.2 89.5 %collective-permute-start.11 = (bf16[1024,1024]{1,0:T(8,128)(2,1)}, bf16[1024,1024]{1,0:T(8,128)(2,1)}, u32[]{:S(2)}, u32[]{:S(2)}) collective-permute-start(bf16[1024,1024]{1,0:T(8,128)(2,1)} %bitcast.21.refs_2_.refs_4_.cot_ref), channel_id=1, source_target_pairs={{0,1},{1,0},{2,3},{3,2},{4,5},{5,4},{6,7},{7,6},{8,9},{9,8},{10,11... | collective-permute-start | bytes 6291464 | tf_op jit(solution)/shard_map/ppermute | solution.py:532
  83.3 49.8 %collective-permute-start.12 = (bf16[1,352,1024]{2,1,0:T(8,128)(2,1)}, bf16[1,352,1024]{2,1,0:T(8,128)(2,1)}, u32[]{:S(2)}, u32[]{:S(2)}) collective-permute-start(bf16[1,352,1024]{2,1,0:T(8,128)(2,1)} %dynamic-slice_bitcast_fusion.9), channel_id=1, source_target_pairs={{0,2},{1,3},{2,0},{3,1},{4,6},{5,7},{6,4},{7,5},{8,10},{9,11},{10,... | collective-permute-start | bytes 2162696 | tf_op jit(solution)/shard_map/ppermute | solution.py:532
  110.3 42.3 %collective-permute-start.8 = (bf16[2,352,1024]{2,1,0:T(8,128)(2,1)}, bf16[2,352,1024]{2,1,0:T(8,128)(2,1)}, u32[]{:S(2)}, u32[]{:S(2)}) collective-permute-start(bf16[2,352,1024]{2,1,0:T(8,128)(2,1)} %dynamic-slice_bitcast_fusion.2), channel_id=1, source_target_pairs={{0,2},{1,3},{2,0},{3,1},{4,6},{5,7},{6,4},{7,5},{8,10},{9,11},{10,... | collective-permute-start | bytes 4325384 | tf_op jit(solution)/shard_map/ppermute | solution.py:532
  133.0 43.3 %collective-permute-start.13 = (bf16[1,352,1024]{2,1,0:T(8,128)(2,1)}, bf16[1,352,1024]{2,1,0:T(8,128)(2,1)}, u32[]{:S(2)}, u32[]{:S(2)}) collective-permute-start(bf16[1,352,1024]{2,1,0:T(8,128)(2,1)} %collective-permute-done.12), channel_id=1, source_target_pairs={{0,8},{4,12},{8,0},{12,4},{16,24},{20,28},{24,16},{28,20},{1,9},{5... | collective-permute-start | bytes 2162696 | tf_op jit(solution)/shard_map/ppermute | solution.py:539
  174.8 87.1 %collective-permute-start.14 = (bf16[3,352,1024]{2,1,0:T(8,128)(2,1)}, bf16[3,352,1024]{2,1,0:T(8,128)(2,1)}, u32[]{:S(2)}, u32[]{:S(2)}) collective-permute-start(bf16[3,352,1024]{2,1,0:T(8,128)(2,1)} %get-tuple-element.201), channel_id=1, source_target_pairs={{0,4},{4,0},{8,12},{12,8},{16,20},{20,16},{24,28},{28,24},{1,5},{5... | collective-permute-start | bytes 6488072 | tf_op jit(solution)/shard_map/ppermute | solution.py:527
  229.0 55.7 %collective-permute-start.15 = (bf16[3,352,1024]{2,1,0:T(8,128)(2,1)}, bf16[3,352,1024]{2,1,0:T(8,128)(2,1)}, u32[]{:S(2)}, u32[]{:S(2)}) collective-permute-start(bf16[3,352,1024]{2,1,0:T(8,128)(2,1)} %get-tuple-element.212), channel_id=1, source_target_pairs={{0,4},{4,0},{8,12},{12,8},{16,20},{20,16},{24,28},{28,24},{1,5},{5... | collective-permute-start | bytes 6488072 | tf_op jit(solution)/shard_map/ppermute | solution.py:527
  246.0 42.1 %collective-permute-start.18 = (bf16[4,8,64,128]{3,2,1,0:T(8,128)(2,1)}, bf16[4,8,64,128]{3,2,1,0:T(8,128)(2,1)S(1)}, u32[]{:S(2)}, u32[]{:S(2)}) collective-permute-start(bf16[4,8,64,128]{3,2,1,0:T(8,128)(2,1)} %get-tuple-element.226), channel_id=1, source_target_pairs={{8,0},{12,4},{16,8},{20,12},{24,16},{28,20},{9,1},{13,5},{17,9},{2... | collective-permute-start | bytes 1572872 | tf_op jit(solution)/shard_map/ppermute | solution.py:527
  261.8 149.7 %reduce-scatter.5.cloned.1.call-start = ((), (), s32[]{:S(2)}) async-start(), calls=%async_computation.5 | async-start | bytes 10485760 | tf_op jit(solution)/shard_map/reduce_scatter | solution.py:944
  287.4 52.1 %collective-permute-start.17 = (bf16[3,352,1024]{2,1,0:T(8,128)(2,1)S(1)}, bf16[3,352,1024]{2,1,0:T(8,128)(2,1)}, u32[]{:S(2)}, u32[]{:S(2)}) collective-permute-start(bf16[3,352,1024]{2,1,0:T(8,128)(2,1)S(1)} %add_convert_fusion.1), channel_id=1, source_target_pairs={{0,2},{1,3},{2,0},{3,1},{4,6},{5,7},{6,4},{7,5},{8,10},{9,11},{10,... | collective-permute-start | bytes 6488072 | tf_op jit(solution)/shard_map/ppermute | solution.py:532
  339.6 205.7 %all-gather.10.cloned.1.call-start = ((), (), s32[]{:S(2)}) async-start(), calls=%async_computation.6 | async-start | bytes 2621440 | tf_op jit(solution)/shard_map/all_gather | solution.py:1045
  345.9 49.0 %collective-permute-start.24 = (bf16[352,1024]{1,0:T(8,128)(2,1)S(1)}, bf16[352,1024]{1,0:T(8,128)(2,1)S(1)}, u32[]{:S(2)}, u32[]{:S(2)}) collective-permute-start(bf16[352,1024]{1,0:T(8,128)(2,1)S(1)} %get-tuple-element.335), channel_id=1, source_target_pairs={{0,8},{4,12},{8,16},{12,20},{16,24},{20,28},{24,0},{28,4},{1,9},{5... | collective-permute-start | bytes 2162696 | tf_op jit(solution)/shard_map/ppermute | solution.py:527
  347.5 61.8 %collective-permute-start.25 = (bf16[352,1024]{1,0:T(8,128)(2,1)S(1)}, bf16[352,1024]{1,0:T(8,128)(2,1)S(1)}, u32[]{:S(2)}, u32[]{:S(2)}) collective-permute-start(bf16[352,1024]{1,0:T(8,128)(2,1)S(1)} %get-tuple-element.334), channel_id=1, source_target_pairs={{0,16},{4,20},{8,24},{12,28},{16,0},{20,4},{24,8},{28,12},{1,17},{... | collective-permute-start | bytes 2162696 | tf_op jit(solution)/shard_map/ppermute | solution.py:527
  348.9 62.4 %collective-permute-start.26 = (bf16[352,1024]{1,0:T(8,128)(2,1)S(1)}, bf16[352,1024]{1,0:T(8,128)(2,1)}, u32[]{:S(2)}, u32[]{:S(2)}) collective-permute-start(bf16[352,1024]{1,0:T(8,128)(2,1)S(1)} %get-tuple-element.333), channel_id=1, source_target_pairs={{0,24},{4,28},{8,0},{12,4},{16,8},{20,12},{24,16},{28,20},{1,25},{... | collective-permute-start | bytes 2162696 | tf_op jit(solution)/shard_map/ppermute | solution.py:527
  418.5 45.9 %collective-permute-start.35 = (bf16[352,1024]{1,0:T(8,128)(2,1)S(1)}, bf16[352,1024]{1,0:T(8,128)(2,1)S(1)}, u32[]{:S(2)}, u32[]{:S(2)}) collective-permute-start(bf16[352,1024]{1,0:T(8,128)(2,1)S(1)} %get-tuple-element.261), channel_id=1, source_target_pairs={{0,4},{4,0},{8,12},{12,8},{16,20},{20,16},{24,28},{28,24},{1,5},{5... | collective-permute-start | bytes 2162696 | tf_op jit(solution)/shard_map/ppermute | solution.py:527
  496.2 45.7 %collective-permute-start.34 = (bf16[480,1024]{1,0:T(8,128)(2,1)}, bf16[480,1024]{1,0:T(8,128)(2,1)}, u32[]{:S(2)}, u32[]{:S(2)}) collective-permute-start(bf16[480,1024]{1,0:T(8,128)(2,1)} %pad_maximum_fusion.6), channel_id=1, source_target_pairs={{0,16},{4,20},{8,24},{12,28},{16,0},{20,4},{24,8},{28,12},{1,17},{... | collective-permute-start | bytes 2949128 | tf_op jit(solution)/shard_map/ppermute | solution.py:527
  502.3 47.9 %collective-permute-start.43 = (bf16[704,1024]{1,0:T(8,128)(2,1)}, bf16[704,1024]{1,0:T(8,128)(2,1)}, u32[]{:S(2)}, u32[]{:S(2)}) collective-permute-start(bf16[704,1024]{1,0:T(8,128)(2,1)} %constant_dynamic-update-slice_fusion.3), channel_id=1, source_target_pairs={{0,4},{4,0},{8,12},{12,8},{16,20},{20,16},{24,28},{28,24},{1,5},{5... | collective-permute-start | bytes 4325384 | tf_op jit(solution)/shard_map/ppermute | solution.py:527
  546.6 45.8 %collective-permute-start.42 = (bf16[352,1024]{1,0:T(8,128)(2,1)}, bf16[352,1024]{1,0:T(8,128)(2,1)}, u32[]{:S(2)}, u32[]{:S(2)}) collective-permute-start(bf16[352,1024]{1,0:T(8,128)(2,1)} %get-tuple-element.283.refs_1_), channel_id=1, source_target_pairs={{0,16},{4,20},{8,24},{12,28},{16,0},{20,4},{24,8},{28,12},{1,17},{... | collective-permute-start | bytes 2162696 | tf_op jit(solution)/shard_map/ppermute | solution.py:527
  594.7 43.2 %collective-permute-start.47 = (bf16[704,1024]{1,0:T(8,128)(2,1)S(1)}, bf16[704,1024]{1,0:T(8,128)(2,1)S(1)}, u32[]{:S(2)}, u32[]{:S(2)}) collective-permute-start(bf16[704,1024]{1,0:T(8,128)(2,1)S(1)} %constant_dynamic-update-slice_fusion.7), channel_id=1, source_target_pairs={{0,4},{4,0},{8,12},{12,8},{16,20},{20,16},{24,28},{28,24},{1,5},{5... | collective-permute-start | bytes 4325384 | tf_op jit(solution)/shard_map/ppermute | solution.py:527
  (83 other events, 1426.6 us)
Sparse Core Ops, SparseCore 0:
  10.9 35.6 all-gather.5
  48.7 34.4 all-gather.7
  84.8 30.0 all-gather.11
  261.9 35.2 reduce-scatter.2
  339.7 71.6 reduce-scatter.4
  500.5 21.5 all-gather.9

commit v3 on v2

--- a/solution.py
+++ b/solution.py
@@ -1075,8 +1075,8 @@
     x_parts = [places.send(x_sent, "quads", k) for k in (1, 2)]
     mix_rows, mix_rest = newton_rows([tied(mix_every, (wide_rows, early_arrived, nearer))], mix_known, own)
     x_pair = jnp.concatenate(tied(x_parts, (mix_rows, nearer_arrived)), axis=0)
-    third = places.send(tied(both, x_pair), "quads", 3)
     x_parts.append(places.send(tied(x_sent, x_pair), "quads", 3))
+    third = places.send(tied(both, x_parts[2]), "quads", 3)
     for k, part in enumerate(x_parts, 1):
         wide_x.add(part, (0, k, 0))
     x_arrived = to_members(x_pair)
@@ -1091,7 +1091,7 @@
     mix_x.add(mix_rest, *[((j - 1) * own, 0, j) for j in range(1, places.members)])
     mix_sent = tied(mix_rows, x_arrived)
     mix_parts = [places.send(mix_sent, "quads", k) for k in (1, 2, 3)]
-    x_last = to_members(tied(x_parts[2], third))
+    x_last = to_members(x_parts[2])
     for j, part in enumerate(x_last, 1):
         wide_x.add(part, (0, 3, j))
     for k, part in enumerate(mix_parts, 1):

time: 714 us -> 711 us (level)
  no operation moved by 1% of the time
where the time goes in v3:
time: 711 us; the launch traced here: 702 us
  Pallas kernels  299 us (42%)
  waiting for transfers between devices  257 us (36%)
  starting transfers between devices  69.5 us (10%)
  other arithmetic  31.9 us (4%)
  local copies, waits for them, and re-layouts  30.1 us (4%)
  between operations  15.2 us (2%)
    ppermute x41, waiting for transfers between devices, send(): return lax.ppermute(value, 'seq', pairs)  185 us
    pallas_call x4, Pallas kernels, ffn(): pl.pallas_call(body, in_specs=[pl.BlockSpec(memory_space=pltpu.SMEM)] * l...  79.2 us
    pallas_call x2, Pallas kernels, newton_rows(): pl.pallas_call(lambda *refs: newton_kernel(len(every), *refs), out_shape=...  64.5 us
    ppermute x41, starting transfers between devices, send(): return lax.ppermute(value, 'seq', pairs)  64.1 us
    all_gather x3, waiting for transfers between devices, gathered(): lax.all_gather(jnp.stack(rows).astype(BF16), 'batch', axis=1, tiled=True)  30.1 us
    pallas_call x4, Pallas kernels, finished(): pl.pallas_call(lambda *refs: finish_kernel(places.members, self.sources,...  29.7 us
    ppermute x10, waiting for transfers between devices, send(): return lax.ppermute(value, 'batch', pairs)  24 us
    pallas_call x1, Pallas kernels, shards(): pl.pallas_call(lambda *refs: att_back_kernel(seqs, *refs), grid=(tiles,),...  22.8 us
  transfers between devices with their start and end apart: 59, of which 28 were waited for; matrix products, arithmetic and copies ran while one was open for 6% of the time, Pallas kernels for 42%

profile of v3, /device:TPU:8, one launch (start us, length us, event | category | flops | bytes accessed | tf_op | source)
XLA Modules:
  0.0 702.3 jit_solution(15115418289256371064)
XLA Ops:
  33.5 13.1 %all-gather.6.cloned.1.call-done.refs_1_.w_ref = bf16[2,1024,1024]{2,1,0:T(8,128)(2,1)} async-done(((bf16[2,256,1024]{2,1,0:T(8,128)(2,1)}), bf16[2,1024,1024]{2,1,0:T(8,128)(2,1)}) %all-gather.6.cloned.1.call-update) | async-done | bytes 4194320 | tf_op jit(solution)/shard_map/all_gather | solution.py:785
  46.6 10.7 %kv.1 = (bf16[1024,1024]{1,0:T(8,128)(2,1)}, bf16[1024,1024]{1,0:T(8,128)(2,1)}, bf16[1024,1024]{1,0:T(8,128)(2,1)}, bf16[1024,1024]{1,0:T(8,128)(2,1)}, bf16[4,8,64,128]{3,2,1,0:T(8,128)(2,1)}) custom-call(bf16[1024,1024]{1,0:T(8,128)(2,1)} %bitcast.139, bf16[2,1024,1024]{2,1,0:T(8,128)(2,1)} %all-gather.6.cloned.1.call-done.refs_1_.w_ref, ...), custom_call_target="tpu_custom_call" | custom-call | flops 42949672960 | bytes 167772160 | tf_op jit(solution)/shard_map/kv/pallas_call | solution.py:824
  66.2 17.0 %all-gather.8.cloned.1.call-done.refs_1_.w_ref = bf16[2,1024,1024]{2,1,0:T(8,128)(2,1)} async-done(((bf16[2,256,1024]{2,1,0:T(8,128)(2,1)}), bf16[2,1024,1024]{2,1,0:T(8,128)(2,1)}) %all-gather.8.cloned.1.call-update) | async-done | bytes 4194320 | tf_op jit(solution)/shard_map/all_gather | solution.py:785
  83.8 15.9 %query.1 = (bf16[1024,1024]{1,0:T(8,128)(2,1)}, bf16[1024,1024]{1,0:T(8,128)(2,1)}, bf16[1024,1024]{1,0:T(8,128)(2,1)}, f32[1024,1024]{1,0:T(8,128)}) custom-call(bf16[1024,1024]{1,0:T(8,128)(2,1)} %get-tuple-element.170.refs_0_.nf_ref.refs_9_.refs_7_, bf16[2,1024,1024]{2,1,0:T(8,128)(2,1)} %all-gather.8.cloned.1.call-done.refs_1_.w_ref, ...), custom_call_target="tpu_custom_call" | custom-call | flops 85899345920 | bytes 167772160 | tf_op jit(solution)/shard_map/query/pallas_call | solution.py:842
  121.3 11.6 %middle.1 = (f32[1024,1024]{1,0:T(8,128)}, bf16[1024,1024]{1,0:T(8,128)(2,1)}, f32[1024,1024]{1,0:T(8,128)}, bf16[1024,1024]{1,0:T(8,128)(2,1)}) custom-call(f32[1024,1024]{1,0:T(8,128)} %get-tuple-element.174.o_ref, bf16[1024,1024]{1,0:T(8,128)(2,1)} %get-tuple-element.175.q_ref.refs_0_, bf16[4,8,64,128]{3,2,1,0:T(8,128)(2,1)} %add_convert_fusion.7.state_ref.refs_7_, ...), custom_call_target="tpu_custom_call" | custom-call | flops 21474836480 | bytes 251658240 | tf_op jit(solution)/shard_map/middle/pallas_call | solution.py:853
  133.1 19.5 %ffn.4 = (f32[1024,1024]{1,0:T(8,128)}, f32[1024,1024]{1,0:T(8,128)}, bf16[3,704,1024]{2,1,0:T(8,128)(2,1)}) custom-call(bf16[1024,1024]{1,0:T(8,128)(2,1)} %get-tuple-element.180.refs_0_.refs_1_, bf16[2,704,1024]{2,1,0:T(8,128)(2,1)} %copy-done.4, bf16[1024,1024]{1,0:T(8,128)(2,1)} %bitcast.21.refs_2_.refs_4_.cot_ref, ...), custom_call_target="tpu_custom_call" | custom-call | flops 118111600640 | bytes 212336640 | tf_op jit(solution)/shard_map/ffn/pallas_call | solution.py:317
  156.0 18.8 %ffn.5 = (f32[1024,1024]{1,0:T(8,128)}, f32[1024,1024]{1,0:T(8,128)}, bf16[3,352,1024]{2,1,0:T(8,128)(2,1)}, bf16[3,352,1024]{2,1,0:T(8,128)(2,1)}) custom-call(bf16[1024,1024]{1,0:T(8,128)(2,1)} %copy-done.41, bf16[2,704,1024]{2,1,0:T(8,128)(2,1)} %copy-done.4, bf16[1024,1024]{1,0:T(8,128)(2,1)} %collective-permute-done.11.refs_2_.refs_4_, ...), custom_call_target="tpu_custom_call" | custom-call | flops 118111600640 | bytes 212336640 | tf_op jit(solution)/shard_map/ffn/pallas_call | solution.py:317
  187.9 19.7 %ffn.6 = (bf16[1024,1024]{1,0:T(8,128)(2,1)}, bf16[1024,1024]{1,0:T(8,128)(2,1)}, bf16[3,704,1024]{2,1,0:T(8,128)(2,1)}) custom-call(s32[1]{0:T(128)} %bitcast.refs_0_, bf16[1024,1024]{1,0:T(8,128)(2,1)} %copy-done.41, bf16[2,352,1024]{2,1,0:T(8,128)(2,1)} %collective-permute-done.8.refs_2_, bf16[2,352,1024]{2,1,0:T(8,128)(2,1)} %copy-done.43, ...), custom_call_target="tpu_custom_call" | custom-call | flops 118111600640 | bytes 212336640 | tf_op jit(solution)/shard_map/ffn/pallas_call | solution.py:317
  207.7 21.2 %ffn.7 = (f32[1024,1024]{1,0:T(8,128)}, f32[1024,1024]{1,0:T(8,128)}, bf16[3,352,1024]{2,1,0:T(8,128)(2,1)}, bf16[3,352,1024]{2,1,0:T(8,128)(2,1)}) custom-call(s32[1]{0:T(128)} %bitcast.refs_0_, bf16[1024,1024]{1,0:T(8,128)(2,1)} %get-tuple-element.180.refs_0_.refs_1_, bf16[2,352,1024]{2,1,0:T(8,128)(2,1)} %collective-permute-done.8.refs_2_, ...), custom_call_target="tpu_custom_call" | custom-call | flops 118111600640 | bytes 212336640 | tf_op jit(solution)/shard_map/ffn/pallas_call | solution.py:317
  231.8 14.1 %gate_back.1 = (bf16[1024,1024]{1,0:T(8,128)(2,1)}, bf16[1024,1024]{1,0:T(8,128)(2,1)}, bf16[1024,1024]{1,0:T(8,128)(2,1)}, bf16[4,8,64,128]{3,2,1,0:T(8,128)(2,1)}) custom-call(f32[1024,1024]{1,0:T(8,128)} %get-tuple-element.212.dn_ref, bf16[1024,1024]{1,0:T(8,128)(2,1)} %copy-done.42, f32[1024,1024]{1,0:T(8,128)} %get-tuple-element.184.refs_4_.mid_ref, ...), custom_call_target="tpu_custom_call" | custom-call | flops 21474836480 | bytes 167772160 | tf_op jit(solution)/shard_map/gate_back/pallas_call | solution.py:896
  261.9 22.8 %attention_back.1 = (bf16[1024,1024]{1,0:T(8,128)(2,1)}, f32[1024,1024]{1,0:T(8,128)}, f32[1024,1024]{1,0:T(8,128)}, bf16[4,1024,1024]{2,1,0:T(8,128)(2,1)}) custom-call(bf16[1024,1024]{1,0:T(8,128)(2,1)} %get-tuple-element.175.q_ref.refs_0_, bf16[1024,1024]{1,0:T(8,128)(2,1)} %get-tuple-element.171.refs_2_.refs_1_.refs_0_, ...), custom_call_target="tpu_custom_call", output_to_operand_aliasing={{3}: (10, {})} | custom-call | flops 85899345920 | bytes 209715200 | tf_op jit(solution)/shard_map/attention_back/pallas_call | solution.py:930
  319.4 12.7 %state_back.1 = (bf16[2,1024,1024]{2,1,0:T(8,128)(2,1)}, bf16[4,1024,1024]{2,1,0:T(8,128)(2,1)}) custom-call(bf16[1024,1024]{1,0:T(8,128)(2,1)} %get-tuple-element.171.refs_2_.refs_1_.refs_0_, bf16[1024,1024]{1,0:T(8,128)(2,1)} %get-tuple-element.172.refs_3_.refs_2_.refs_1_, ...), custom_call_target="tpu_custom_call", output_to_operand_aliasing={{1}: (8, {})} | custom-call | flops 53687091200 | bytes 188743680 | tf_op jit(solution)/shard_map/state_back/pallas_call | solution.py:971
  354.8 11.0 %input_back.1 = bf16[1024,1024]{1,0:T(8,128)(2,1)} custom-call(bf16[2,1024,1024]{2,1,0:T(8,128)(2,1)} %get-tuple-element.239.dkv_ref, bf16[2,1024,1024]{2,1,0:T(8,128)(2,1)} %all-gather.6.cloned.1.call-done.refs_1_.w_ref, f32[1024,1024]{1,0:T(8,128)} %normed_back.1.part_ref, bf16[1024,1024]{1,0:T(8,128)(2,1)} %bitcast.141, ...), custom_call_target="tpu_custom_call" | custom-call | flops 42949672960 | bytes 167772160 | tf_op jit(solution)/shard_map/input_back/pallas_call | solution.py:991
  365.7 29.2 %collective-permute-done.24 = bf16[352,1024]{1,0:T(8,128)(2,1)S(1)} collective-permute-done((bf16[352,1024]{1,0:T(8,128)(2,1)S(1)}, bf16[352,1024]{1,0:T(8,128)(2,1)S(1)}, u32[]{:S(2)}, u32[]{:S(2)}) %collective-permute-start.24) | collective-permute-done | bytes 720928 | tf_op jit(solution)/shard_map/ppermute | solution.py:527
  394.9 14.3 %collective-permute-done.25 = bf16[352,1024]{1,0:T(8,128)(2,1)S(1)} collective-permute-done((bf16[352,1024]{1,0:T(8,128)(2,1)S(1)}, bf16[352,1024]{1,0:T(8,128)(2,1)S(1)}, u32[]{:S(2)}, u32[]{:S(2)}) %collective-permute-start.25) | collective-permute-done | bytes 720928 | tf_op jit(solution)/shard_map/ppermute | solution.py:527
  419.0 16.5 %collective-permute-done.28 = bf16[352,1024]{1,0:T(8,128)(2,1)S(1)} collective-permute-done((bf16[352,1024]{1,0:T(8,128)(2,1)S(1)}, bf16[352,1024]{1,0:T(8,128)(2,1)S(1)}, u32[]{:S(2)}, u32[]{:S(2)}) %collective-permute-start.28) | collective-permute-done | bytes 720928 | tf_op jit(solution)/shard_map/ppermute | solution.py:532
  444.7 14.7 %collective-permute-done.29 = bf16[128,1024]{1,0:T(8,128)(2,1)S(1)} collective-permute-done((bf16[128,1024]{1,0:T(8,128)(2,1)S(1)}, bf16[128,1024]{1,0:T(8,128)(2,1)S(1)}, u32[]{:S(2)}, u32[]{:S(2)}) %collective-permute-start.29) | collective-permute-done | bytes 262176 | tf_op jit(solution)/shard_map/ppermute | solution.py:527
  478.8 17.4 %collective-permute-done.33.refs_4_ = bf16[128,1024]{1,0:T(8,128)(2,1)S(1)} collective-permute-done((bf16[128,1024]{1,0:T(8,128)(2,1)S(1)}, bf16[128,1024]{1,0:T(8,128)(2,1)S(1)}, u32[]{:S(2)}, u32[]{:S(2)}) %collective-permute-start.33) | collective-permute-done | bytes 262176 | tf_op jit(solution)/shard_map/ppermute | solution.py:527
  504.6 37.3 %newton.2 = (bf16[352,1024]{1,0:T(8,128)(2,1)}, bf16[352,1024]{1,0:T(8,128)(2,1)}) custom-call(bf16[1056,1024]{1,0:T(8,128)(2,1)} %constant_dynamic-update-slice_fusion.refs_0_, bf16[1056,1024]{1,0:T(8,128)(2,1)} %collective-permute-done.37.refs_1_, bf16[352,1024]{1,0:T(8,128)(2,1)} %copy-done.44, bf16[352,1024]{1,0:T(8,128)(2,1)} %copy-done.45, ...), custom_call_target="tpu_custom_call" | custom-call | flops 412048424960 | bytes 86507520 | tf_op jit(solution)/shard_map/newton/pallas_call | solution.py:481
  550.1 27.2 %newton.3 = (bf16[128,1024]{1,0:T(8,128)(2,1)}, bf16[128,1024]{1,0:T(8,128)(2,1)}) custom-call(bf16[1024,1024]{1,0:T(8,128)(2,1)} %all-gather.10.cloned.1.call-done.refs_0_, bf16[256,1024]{1,0:T(8,128)(2,1)} %pad_maximum_fusion.8.refs_1_), custom_call_target="tpu_custom_call" | custom-call | flops 327491256320 | bytes 31457280 | tf_op jit(solution)/shard_map/newton/pallas_call | solution.py:481
  577.4 15.0 %collective-permute-done.42.refs_4_ = bf16[352,1024]{1,0:T(8,128)(2,1)} collective-permute-done((bf16[352,1024]{1,0:T(8,128)(2,1)}, bf16[352,1024]{1,0:T(8,128)(2,1)}, u32[]{:S(2)}, u32[]{:S(2)}) %collective-permute-start.42) | collective-permute-done | bytes 720928 | tf_op jit(solution)/shard_map/ppermute | solution.py:527
  600.7 14.4 %collective-permute-done.44.refs_5_ = bf16[352,1024]{1,0:T(8,128)(2,1)S(1)} collective-permute-done((bf16[352,1024]{1,0:T(8,128)(2,1)}, bf16[352,1024]{1,0:T(8,128)(2,1)S(1)}, u32[]{:S(2)}, u32[]{:S(2)}) %collective-permute-start.44) | collective-permute-done | bytes 720928 | tf_op jit(solution)/shard_map/ppermute | solution.py:527
  618.0 16.6 %collective-permute-done.47.refs_6_ = bf16[704,1024]{1,0:T(8,128)(2,1)S(1)} collective-permute-done((bf16[704,1024]{1,0:T(8,128)(2,1)S(1)}, bf16[704,1024]{1,0:T(8,128)(2,1)S(1)}, u32[]{:S(2)}, u32[]{:S(2)}) %collective-permute-start.47) | collective-permute-done | bytes 1441824 | tf_op jit(solution)/shard_map/ppermute | solution.py:527
  637.1 13.2 %collective-permute-done.45.refs_6_ = bf16[480,1024]{1,0:T(8,128)(2,1)S(1)} collective-permute-done((bf16[480,1024]{1,0:T(8,128)(2,1)}, bf16[480,1024]{1,0:T(8,128)(2,1)S(1)}, u32[]{:S(2)}, u32[]{:S(2)}) %collective-permute-start.45) | collective-permute-done | bytes 983072 | tf_op jit(solution)/shard_map/ppermute | solution.py:527
  (279 shorter events, 263.3 us)
Async XLA Ops:
  7.2 39.4 %all-gather.6.cloned.1.call-start = ((), (), s32[]{:S(2)}) async-start(), calls=%async_computation.2 | async-start | bytes 5242880 | tf_op jit(solution)/shard_map/all_gather | solution.py:785
  10.8 72.4 %all-gather.8.cloned.1.call-start = ((), (), s32[]{:S(2)}) async-start(), calls=%async_computation.3 | async-start | bytes 5242880 | tf_op jit(solution)/shard_map/all_gather | solution.py:785
  12.0 109.3 %all-gather.12.cloned.1.call-start = ((), (), s32[]{:S(2)}) async-start(), calls=%async_computation.7 | async-start | bytes 2621440 | tf_op jit(solution)/shard_map/all_gather | solution.py:785
  22.0 275.2 %reduce-scatter.3.cloned.1.call-start = ((), (), s32[]{:S(2)}) async-start(), calls=%async_computation.4 | async-start | bytes 2621440 | tf_op jit(solution)/shard_map/reduce_scatter | solution.py:944
  57.3 42.5 %collective-permute-start.4 = (bf16[4,8,64,128]{3,2,1,0:T(8,128)(2,1)}, bf16[4,8,64,128]{3,2,1,0:T(8,128)(2,1)S(1)}, u32[]{:S(2)}, u32[]{:S(2)}) collective-permute-start(bf16[4,8,64,128]{3,2,1,0:T(8,128)(2,1)} %get-tuple-element.177), channel_id=1, source_target_pairs={{0,8},{4,12},{8,16},{12,20},{16,24},{20,28},{1,9},{5,13},{9,17},{1... | collective-permute-start | bytes 1572872 | tf_op jit(solution)/shard_map/ppermute | solution.py:527
  60.7 45.6 %collective-permute-start.5 = (bf16[4,8,64,128]{3,2,1,0:T(8,128)(2,1)}, bf16[4,8,64,128]{3,2,1,0:T(8,128)(2,1)S(1)}, u32[]{:S(2)}, u32[]{:S(2)}) collective-permute-start(bf16[4,8,64,128]{3,2,1,0:T(8,128)(2,1)} %get-tuple-element.177), channel_id=1, source_target_pairs={{0,16},{4,20},{8,24},{12,28},{1,17},{5,21},{9,25},{13,29},{2,18},{... | collective-permute-start | bytes 1572872 | tf_op jit(solution)/shard_map/ppermute | solution.py:527
  62.9 43.3 %collective-permute-start.6 = (bf16[4,8,64,128]{3,2,1,0:T(8,128)(2,1)}, bf16[4,8,64,128]{3,2,1,0:T(8,128)(2,1)S(1)}, u32[]{:S(2)}, u32[]{:S(2)}) collective-permute-start(bf16[4,8,64,128]{3,2,1,0:T(8,128)(2,1)} %get-tuple-element.177), channel_id=1, source_target_pairs={{0,24},{4,28},{1,25},{5,29},{2,26},{6,30},{3,27},{7,31}} | collective-permute-start | bytes 1572872 | tf_op jit(solution)/shard_map/ppermute | solution.py:527
  65.2 89.5 %collective-permute-start.11 = (bf16[1024,1024]{1,0:T(8,128)(2,1)}, bf16[1024,1024]{1,0:T(8,128)(2,1)}, u32[]{:S(2)}, u32[]{:S(2)}) collective-permute-start(bf16[1024,1024]{1,0:T(8,128)(2,1)} %bitcast.21.refs_2_.refs_4_.cot_ref), channel_id=1, source_target_pairs={{0,1},{1,0},{2,3},{3,2},{4,5},{5,4},{6,7},{7,6},{8,9},{9,8},{10,11... | collective-permute-start | bytes 6291464 | tf_op jit(solution)/shard_map/ppermute | solution.py:532
  83.3 49.8 %collective-permute-start.12 = (bf16[1,352,1024]{2,1,0:T(8,128)(2,1)}, bf16[1,352,1024]{2,1,0:T(8,128)(2,1)}, u32[]{:S(2)}, u32[]{:S(2)}) collective-permute-start(bf16[1,352,1024]{2,1,0:T(8,128)(2,1)} %dynamic-slice_bitcast_fusion.9), channel_id=1, source_target_pairs={{0,2},{1,3},{2,0},{3,1},{4,6},{5,7},{6,4},{7,5},{8,10},{9,11},{10,... | collective-permute-start | bytes 2162696 | tf_op jit(solution)/shard_map/ppermute | solution.py:532
  110.3 42.3 %collective-permute-start.8 = (bf16[2,352,1024]{2,1,0:T(8,128)(2,1)}, bf16[2,352,1024]{2,1,0:T(8,128)(2,1)}, u32[]{:S(2)}, u32[]{:S(2)}) collective-permute-start(bf16[2,352,1024]{2,1,0:T(8,128)(2,1)} %dynamic-slice_bitcast_fusion.2), channel_id=1, source_target_pairs={{0,2},{1,3},{2,0},{3,1},{4,6},{5,7},{6,4},{7,5},{8,10},{9,11},{10,... | collective-permute-start | bytes 4325384 | tf_op jit(solution)/shard_map/ppermute | solution.py:532
  133.0 43.3 %collective-permute-start.13 = (bf16[1,352,1024]{2,1,0:T(8,128)(2,1)}, bf16[1,352,1024]{2,1,0:T(8,128)(2,1)}, u32[]{:S(2)}, u32[]{:S(2)}) collective-permute-start(bf16[1,352,1024]{2,1,0:T(8,128)(2,1)} %collective-permute-done.12), channel_id=1, source_target_pairs={{0,8},{4,12},{8,0},{12,4},{16,24},{20,28},{24,16},{28,20},{1,9},{5... | collective-permute-start | bytes 2162696 | tf_op jit(solution)/shard_map/ppermute | solution.py:539
  174.8 87.1 %collective-permute-start.14 = (bf16[3,352,1024]{2,1,0:T(8,128)(2,1)}, bf16[3,352,1024]{2,1,0:T(8,128)(2,1)}, u32[]{:S(2)}, u32[]{:S(2)}) collective-permute-start(bf16[3,352,1024]{2,1,0:T(8,128)(2,1)} %get-tuple-element.200), channel_id=1, source_target_pairs={{0,4},{4,0},{8,12},{12,8},{16,20},{20,16},{24,28},{28,24},{1,5},{5... | collective-permute-start | bytes 6488072 | tf_op jit(solution)/shard_map/ppermute | solution.py:527
  229.0 55.7 %collective-permute-start.15 = (bf16[3,352,1024]{2,1,0:T(8,128)(2,1)}, bf16[3,352,1024]{2,1,0:T(8,128)(2,1)}, u32[]{:S(2)}, u32[]{:S(2)}) collective-permute-start(bf16[3,352,1024]{2,1,0:T(8,128)(2,1)} %get-tuple-element.211), channel_id=1, source_target_pairs={{0,4},{4,0},{8,12},{12,8},{16,20},{20,16},{24,28},{28,24},{1,5},{5... | collective-permute-start | bytes 6488072 | tf_op jit(solution)/shard_map/ppermute | solution.py:527
  246.0 42.1 %collective-permute-start.18 = (bf16[4,8,64,128]{3,2,1,0:T(8,128)(2,1)}, bf16[4,8,64,128]{3,2,1,0:T(8,128)(2,1)S(1)}, u32[]{:S(2)}, u32[]{:S(2)}) collective-permute-start(bf16[4,8,64,128]{3,2,1,0:T(8,128)(2,1)} %get-tuple-element.225), channel_id=1, source_target_pairs={{8,0},{12,4},{16,8},{20,12},{24,16},{28,20},{9,1},{13,5},{17,9},{2... | collective-permute-start | bytes 1572872 | tf_op jit(solution)/shard_map/ppermute | solution.py:527
  261.8 149.7 %reduce-scatter.5.cloned.1.call-start = ((), (), s32[]{:S(2)}) async-start(), calls=%async_computation.5 | async-start | bytes 10485760 | tf_op jit(solution)/shard_map/reduce_scatter | solution.py:944
  287.4 52.1 %collective-permute-start.17 = (bf16[3,352,1024]{2,1,0:T(8,128)(2,1)S(1)}, bf16[3,352,1024]{2,1,0:T(8,128)(2,1)}, u32[]{:S(2)}, u32[]{:S(2)}) collective-permute-start(bf16[3,352,1024]{2,1,0:T(8,128)(2,1)S(1)} %add_convert_fusion.1), channel_id=1, source_target_pairs={{0,2},{1,3},{2,0},{3,1},{4,6},{5,7},{6,4},{7,5},{8,10},{9,11},{10,... | collective-permute-start | bytes 6488072 | tf_op jit(solution)/shard_map/ppermute | solution.py:532
  339.6 205.7 %all-gather.10.cloned.1.call-start = ((), (), s32[]{:S(2)}) async-start(), calls=%async_computation.6 | async-start | bytes 2621440 | tf_op jit(solution)/shard_map/all_gather | solution.py:1045
  345.9 49.0 %collective-permute-start.24 = (bf16[352,1024]{1,0:T(8,128)(2,1)S(1)}, bf16[352,1024]{1,0:T(8,128)(2,1)S(1)}, u32[]{:S(2)}, u32[]{:S(2)}) collective-permute-start(bf16[352,1024]{1,0:T(8,128)(2,1)S(1)} %get-tuple-element.333), channel_id=1, source_target_pairs={{0,8},{4,12},{8,16},{12,20},{16,24},{20,28},{24,0},{28,4},{1,9},{5... | collective-permute-start | bytes 2162696 | tf_op jit(solution)/shard_map/ppermute | solution.py:527
  347.5 61.8 %collective-permute-start.25 = (bf16[352,1024]{1,0:T(8,128)(2,1)S(1)}, bf16[352,1024]{1,0:T(8,128)(2,1)S(1)}, u32[]{:S(2)}, u32[]{:S(2)}) collective-permute-start(bf16[352,1024]{1,0:T(8,128)(2,1)S(1)} %get-tuple-element.332), channel_id=1, source_target_pairs={{0,16},{4,20},{8,24},{12,28},{16,0},{20,4},{24,8},{28,12},{1,17},{... | collective-permute-start | bytes 2162696 | tf_op jit(solution)/shard_map/ppermute | solution.py:527
  348.9 62.4 %collective-permute-start.26 = (bf16[352,1024]{1,0:T(8,128)(2,1)S(1)}, bf16[352,1024]{1,0:T(8,128)(2,1)}, u32[]{:S(2)}, u32[]{:S(2)}) collective-permute-start(bf16[352,1024]{1,0:T(8,128)(2,1)S(1)} %get-tuple-element.331), channel_id=1, source_target_pairs={{0,24},{4,28},{8,0},{12,4},{16,8},{20,12},{24,16},{28,20},{1,25},{... | collective-permute-start | bytes 2162696 | tf_op jit(solution)/shard_map/ppermute | solution.py:527
  418.5 45.9 %collective-permute-start.35 = (bf16[352,1024]{1,0:T(8,128)(2,1)S(1)}, bf16[352,1024]{1,0:T(8,128)(2,1)S(1)}, u32[]{:S(2)}, u32[]{:S(2)}) collective-permute-start(bf16[352,1024]{1,0:T(8,128)(2,1)S(1)} %get-tuple-element.260), channel_id=1, source_target_pairs={{0,4},{4,0},{8,12},{12,8},{16,20},{20,16},{24,28},{28,24},{1,5},{5... | collective-permute-start | bytes 2162696 | tf_op jit(solution)/shard_map/ppermute | solution.py:527
  496.2 45.7 %collective-permute-start.34 = (bf16[480,1024]{1,0:T(8,128)(2,1)}, bf16[480,1024]{1,0:T(8,128)(2,1)}, u32[]{:S(2)}, u32[]{:S(2)}) collective-permute-start(bf16[480,1024]{1,0:T(8,128)(2,1)} %pad_maximum_fusion.6), channel_id=1, source_target_pairs={{0,16},{4,20},{8,24},{12,28},{16,0},{20,4},{24,8},{28,12},{1,17},{... | collective-permute-start | bytes 2949128 | tf_op jit(solution)/shard_map/ppermute | solution.py:527
  502.3 47.9 %collective-permute-start.43 = (bf16[704,1024]{1,0:T(8,128)(2,1)}, bf16[704,1024]{1,0:T(8,128)(2,1)}, u32[]{:S(2)}, u32[]{:S(2)}) collective-permute-start(bf16[704,1024]{1,0:T(8,128)(2,1)} %constant_dynamic-update-slice_fusion.3), channel_id=1, source_target_pairs={{0,4},{4,0},{8,12},{12,8},{16,20},{20,16},{24,28},{28,24},{1,5},{5... | collective-permute-start | bytes 4325384 | tf_op jit(solution)/shard_map/ppermute | solution.py:527
  546.6 45.8 %collective-permute-start.42 = (bf16[352,1024]{1,0:T(8,128)(2,1)}, bf16[352,1024]{1,0:T(8,128)(2,1)}, u32[]{:S(2)}, u32[]{:S(2)}) collective-permute-start(bf16[352,1024]{1,0:T(8,128)(2,1)} %get-tuple-element.281.refs_1_), channel_id=1, source_target_pairs={{0,16},{4,20},{8,24},{12,28},{16,0},{20,4},{24,8},{28,12},{1,17},{... | collective-permute-start | bytes 2162696 | tf_op jit(solution)/shard_map/ppermute | solution.py:527
  (83 other events, 1417.0 us)
Sparse Core Ops, SparseCore 0:
  10.9 35.6 all-gather.5
  48.7 34.4 all-gather.7
  84.8 30.0 all-gather.11
  261.9 35.2 reduce-scatter.2
  339.7 71.6 reduce-scatter.4
  500.5 21.5 all-gather.9
